TPU v7x, 768 devices: a whole 4x8x12 slice. The times are simulated.
768 devices in a mesh: grp: 96 (over x, z, core), sub: 8 (over y).
Axes of the slice: x: 4, y: 8, z: 12, core: 2. Of those that a mesh axis runs over, the one named last changes fastest.
Arguments:
- ocean_state: bfloat16 [8, 3145728], P(None, ('grp', 'sub')), may hold values from -6 to 6
- ocean_area: float32 [3145728], P(('grp', 'sub')), may hold values from 0.3 to 3
- atm_flux: bfloat16 [12, 786432], P(None, ('grp', 'sub')), may hold values from -6 to 6
- atm_area: float32 [786432], P(('grp', 'sub')), may hold values from 0.3 to 3
- coupling: float32 [12, 8], replicated, may hold values from -2 to 2
- remap_weight: bfloat16 [6144, 12, 128, 128], P(('grp', 'sub')), may hold values from -0.21875 to 0.21875
- send_block: int32 [768, 3, 8, 6], P(('grp', 'sub')), may hold values from 0 to 31
- send_count: int32 [768, 3, 8], P(('grp', 'sub')), may hold values from 2 to 6, as said below
- link_slot: int32 [6144, 12], P(('grp', 'sub')), may hold values from 0 to 143, as said below
- link_count: int32 [6144], P(('grp', 'sub')), may hold values from 1 to 12, as said below
Outputs:
- state_on_atm: bfloat16 [8, 786432], P(None, ('grp', 'sub'))
- flux_on_ocean: bfloat16 [12, 3145728], P(None, ('grp', 'sub'))
- imbalance: float32 [12], replicated
Inputs may be any that keep to these rules, and one draw needn't show every extreme that they name: `send_count`: every rank has one route with exactly 6 live slots. `link_slot`: the 12 slots of one atmosphere block differ, and each is a live slot of the sending route. `link_count`: every rank has an atmosphere block with all 12 links live.
All inputs are finite; a program needn't handle non-finite values.
Results may differ from a plain program's by a relative error of at most 0.0075.
Values may be sent and summed in bfloat16 or wider, within the bound.
No kernel may reach another device: no remote copies, remote signals or barrier semaphores. Data moves between devices by JAX's collectives and lax.ppermute only.
A program may use at most 32 MiB of HBM per device.

v0:
```python
import math

import jax
import jax.numpy as jnp
from jax import lax
from jax.sharding import PartitionSpec as P


def extended(block, sides, width):
    for axis, dim in sides:
        count = lax.axis_size(axis)
        forward = [(i, i + 1) for i in range(count - 1)]
        forward.append((count - 1, 0))
        backward = [(target, source) for source, target in forward]
        low = lax.ppermute(
            lax.slice_in_dim(block, block.shape[dim] - width, None, axis=dim), axis, forward
        )
        high = lax.ppermute(lax.slice_in_dim(block, 0, width, axis=dim), axis, backward)
        block = jnp.concatenate([low, block, high], axis=dim)
    return block


def state_across(routed):
    wider = extended(routed, (("grp", 0),), 1)
    return wider[0::2]


def state_within(routed):
    return lax.all_to_all(routed, "sub", split_axis=1, concat_axis=1, tiled=True)


def flux_across(partial_value):
    wider = extended(partial_value, (("grp", 0),), 1)
    return wider[0::2]


def flux_within(partial_value):
    return lax.all_to_all(partial_value, "sub", split_axis=1, concat_axis=1, tiled=True)


def shards(
    ocean_state,
    ocean_area,
    atm_flux,
    atm_area,
    coupling,
    remap_weight,
    send_block,
    send_count,
    link_slot,
    link_count,
):
    fields_ocean = ocean_state.shape[0]
    fields_atm = atm_flux.shape[0]
    atm_blocks = remap_weight.shape[0]
    link_total = remap_weight.shape[1]
    width = remap_weight.shape[2]
    ocean_blocks = ocean_state.shape[1] // width
    route_subs = send_block.shape[2]
    capacity = send_block.shape[3]
    slot_total = 3 * route_subs * capacity
    slot_index = lax.broadcasted_iota(jnp.int32, send_block.shape, 3)
    alive_slot = slot_index < send_count[:, :, :, None]
    chosen = jnp.where(alive_slot, send_block, -1).reshape(slot_total)
    chooser = (chosen[:, None] == jnp.arange(ocean_blocks, dtype=jnp.int32)[None, :]).astype(
        jnp.bfloat16
    )
    ocean_blocked = ocean_state.reshape(fields_ocean, ocean_blocks, width)
    routed = jnp.einsum(
        "sb,fbr->sfr", chooser, ocean_blocked, preferred_element_type=jnp.float32
    ).astype(jnp.bfloat16)
    routed = routed.reshape(3, route_subs, capacity, fields_ocean, width)
    arrived = state_within(state_across(routed))
    received = arrived.reshape(slot_total, fields_ocean, width)
    link_flat = link_slot.reshape(-1)
    taken = jnp.take(received, link_flat, axis=0).reshape(
        atm_blocks, link_total, fields_ocean, width
    )
    used_link = lax.broadcasted_iota(jnp.int32, link_slot.shape, 1) < link_count[:, None]
    taken = jnp.where(used_link[:, :, None, None], taken, jnp.zeros((), jnp.bfloat16))
    state_sum = jnp.einsum(
        "alfr,alrq->faq", taken, remap_weight, preferred_element_type=jnp.float32
    )
    flux_blocked = atm_flux.reshape(fields_atm, atm_blocks, width)
    coupled = (
        flux_blocked.astype(jnp.float32)
        + jnp.einsum("gf,faq->gaq", coupling, state_sum, precision=lax.Precision.HIGHEST)
    ).astype(jnp.bfloat16)
    link_part = jnp.einsum(
        "gaq,alrq->algr", coupled, remap_weight, preferred_element_type=jnp.float32
    )
    slot_hits = (
        link_flat[None, :] == jnp.arange(slot_total, dtype=jnp.int32)[:, None]
    ) & used_link.reshape(-1)[None, :]
    slot_hits = slot_hits.astype(jnp.float32)
    slot_part = jnp.dot(
        slot_hits,
        link_part.reshape(atm_blocks * link_total, fields_atm * width),
        precision=lax.Precision.HIGHEST,
    ).astype(jnp.bfloat16)
    slot_part = slot_part.reshape(3, route_subs, capacity, fields_atm, width)
    returned = flux_across(flux_within(slot_part))
    flux_sum = jnp.einsum(
        "sb,sgr->gbr",
        chooser,
        returned.reshape(slot_total, fields_atm, width),
        preferred_element_type=jnp.float32,
    )
    atm_part = jnp.sum(
        atm_area.reshape(atm_blocks, width)[None] * coupled.astype(jnp.float32), axis=(1, 2)
    )
    ocean_part = jnp.sum(ocean_area.reshape(ocean_blocks, width)[None] * flux_sum, axis=(1, 2))
    atm_total, ocean_total = lax.psum((atm_part, ocean_part), ("grp", "sub"))
    devices_all = lax.axis_size("grp") * lax.axis_size("sub")
    norm_scale = 1.0 / math.sqrt(devices_all * atm_blocks * width)
    imbalance = (atm_total - ocean_total) * norm_scale
    state_on_atm = state_sum.reshape(fields_ocean, atm_blocks * width).astype(jnp.bfloat16)
    flux_on_ocean = flux_sum.reshape(fields_atm, ocean_blocks * width).astype(jnp.bfloat16)
    return (state_on_atm, flux_on_ocean, imbalance)


def solution(mesh):
    placed = (
        P(None, ("grp", "sub")),
        P(("grp", "sub")),
        P(None, ("grp", "sub")),
        P(("grp", "sub")),
        P(),
        P(("grp", "sub"), None, None, None),
        P(("grp", "sub"), None, None, None),
        P(("grp", "sub"), None, None),
        P(("grp", "sub"), None),
        P(("grp", "sub")),
    )
    return jax.shard_map(
        shards,
        mesh=mesh,
        in_specs=placed,
        out_specs=(P(None, ("grp", "sub")), P(None, ("grp", "sub")), P()),
        check_vma=False,
    )
```

profile of v0, /device:TPU:1, one launch (start us, length us, event | category | flops | bytes accessed | tf_op | source)
XLA Modules:
  0.0 201.7 jit_solution(4526959713903309907)
XLA Ops:
  0.7 0.8 copy.48
  1.5 0.8 compare_select_fusion
  2.5 1.1 convolution_convert_fusion.1
  3.7 12.4 %collective-permute-start.1 = (bf16[1,8,6,8,128]{4,3,2,1,0:T(8,128)(2,1)S(1)}, bf16[1,8,6,8,128]{4,3,2,1,0:T(8,128)(2,1)}, u32[]{:S(2)}, u32[]{:S(2)}) collective-permute-start(bf16[1,8,6,8,128]{4,3,2,1,0:T(8,128)(2,1)S(1)} %bitcast.72), channel_id=1, source_target_pairs={{8,0},{16,8},{24,16},{32,24},{40,32},{48,40},{56,48},{64,56},{72,6... | collective-permute-start | bytes 294920 | tf_op jit(solution)/shard_map/ppermute | solution.py:18
  16.8 1.9 collective-permute-start
  18.7 0.8 reshape.127
  19.5 0.8 reshape.126
  20.4 4.8 %collective-permute-done = bf16[1,8,6,8,128]{4,3,2,1,0:T(8,128)(2,1)} collective-permute-done((bf16[1,8,6,8,128]{4,3,2,1,0:T(8,128)(2,1)}, bf16[1,8,6,8,128]{4,3,2,1,0:T(8,128)(2,1)}, u32[]{:S(2)}, u32[]{:S(2)}) %collective-permute-start) | collective-permute-done | bytes 98336 | tf_op jit(solution)/shard_map/ppermute | solution.py:15
  25.1 1.0 pad_maximum_fusion.1
  26.9 6.8 %all-to-all-start = ((bf16[3,8,6,8,128]{4,3,2,0,1:T(8,128)(2,1)}), bf16[3,8,6,8,128]{4,3,2,0,1:T(8,128)(2,1)S(1)}, u32[]{:S(2)}, u32[]{:S(2)}) async-start(bf16[3,8,6,8,128]{4,3,2,0,1:T(8,128)(2,1)} %copy.29), calls=%async_computation | async-start | bytes 589824 | tf_op jit(solution)/shard_map/all_to_all | solution.py:29
  34.6 0.8 convert_element_type.42
  35.4 8.0 %all-to-all-done = bf16[3,8,6,8,128]{4,3,2,0,1:T(8,128)(2,1)S(1)} async-done(((bf16[3,8,6,8,128]{4,3,2,0,1:T(8,128)(2,1)}), bf16[3,8,6,8,128]{4,3,2,0,1:T(8,128)(2,1)S(1)}, u32[]{:S(2)}, u32[]{:S(2)}) %all-to-all-start) | async-done | bytes 294944 | tf_op jit(solution)/shard_map/all_to_all | solution.py:29
  44.2 1.6 gather_fusion
  46.8 0.9 fusion.15
  47.7 1.5 convolution_convert_fusion
  49.2 2.1 %reshape.129 = bf16[3,8,6,12,128]{4,3,2,1,0:T(8,128)(2,1)} reshape(bf16[144,1536]{1,0:T(8,128)(2,1)} %convolution_convert_fusion) | data formatting | bytes 884736 | tf_op jit(solution)/shard_map/reshape | solution.py:101
  51.3 1.1 copy.32
  52.5 15.2 %all_to_all.10 = bf16[3,8,6,12,128]{4,3,2,0,1:T(8,128)(2,1)S(1)} all-to-all(bf16[3,8,6,12,128]{4,3,2,0,1:T(8,128)(2,1)S(1)} %copy.32), channel_id=1, replica_groups=mesh['grp'=96,'sub'=8] {'sub'}, dimensions={1} | all-to-all | bytes 884736 | tf_op jit(solution)/shard_map/all_to_all | solution.py:38
  67.7 1.9 collective-permute-start.2
  69.6 11.0 %collective-permute-start.3 = (bf16[1,8,6,12,128]{4,3,2,0,1:T(8,128)(2,1)S(1)}, bf16[1,8,6,12,128]{4,3,2,0,1:T(8,128)(2,1)S(1)}, u32[]{:S(2)}, u32[]{:S(2)}) collective-permute-start(bf16[1,8,6,12,128]{4,3,2,0,1:T(8,128)(2,1)S(1)} %get-tuple-element.6), channel_id=1, source_target_pairs={{8,0},{16,8},{24,16},{32,24},{40,32},{48,40},{56,48},{64,56},{72,6... | collective-permute-start | bytes 442376 | tf_op jit(solution)/shard_map/ppermute | solution.py:18
  82.0 1.0 copy.33
  82.9 2.0 reshape.130
  84.9 1.3 multiply_reduce_fusion
  87.0 114.2 %all-reduce = (f32[12]{0:T(128)S(1)}, f32[12]{0:T(128)S(1)}) all-reduce(f32[12]{0:T(128)S(1)} %get-tuple-element.12, f32[12]{0:T(128)S(1)} %get-tuple-element.9), channel_id=1, replica_groups=mesh['grp'=96,'sub'=8] {'grp','sub'}, use_global_device_ids=true, to_apply=%region_1.2 | all-reduce | flops 24 | bytes 192 | tf_op jit(solution)/shard_map/psum | solution.py:113
  (37 shorter events, 6.9 us)
Async XLA Ops:
  0.6 45.2 %copy-start = (bf16[8,12,128,128]{3,2,1,0:T(8,128)(2,1)S(1)}, bf16[8,12,128,128]{3,2,1,0:T(8,128)(2,1)}, u32[]{:S(2)}) copy-start(bf16[8,12,128,128]{3,2,1,0:T(8,128)(2,1)} %param.15) | copy-start | bytes 9437188
  0.6 33.1 %copy-start.1 = (s32[8,12]{1,0:T(8,128)S(1)}, s32[8,12]{1,0:T(8,128)}, u32[]{:S(2)}) copy-start(s32[8,12]{1,0:T(8,128)} %param.18) | copy-start | bytes 1156
  3.7 16.6 %collective-permute-start.1 = (bf16[1,8,6,8,128]{4,3,2,1,0:T(8,128)(2,1)S(1)}, bf16[1,8,6,8,128]{4,3,2,1,0:T(8,128)(2,1)}, u32[]{:S(2)}, u32[]{:S(2)}) collective-permute-start(bf16[1,8,6,8,128]{4,3,2,1,0:T(8,128)(2,1)S(1)} %bitcast.72), channel_id=1, source_target_pairs={{8,0},{16,8},{24,16},{32,24},{40,32},{48,40},{56,48},{64,56},{72,6... | collective-permute-start | bytes 294920 | tf_op jit(solution)/shard_map/ppermute | solution.py:18
  16.8 8.3 %collective-permute-start = (bf16[1,8,6,8,128]{4,3,2,1,0:T(8,128)(2,1)}, bf16[1,8,6,8,128]{4,3,2,1,0:T(8,128)(2,1)}, u32[]{:S(2)}, u32[]{:S(2)}) collective-permute-start(bf16[1,8,6,8,128]{4,3,2,1,0:T(8,128)(2,1)} %bitcast.2), channel_id=1, source_target_pairs={{0,8},{8,16},{16,24},{24,32},{32,40},{40,48},{48,56},{56,64},{64,7... | collective-permute-start | bytes 294920 | tf_op jit(solution)/shard_map/ppermute | solution.py:15
  26.2 20.2 %copy-start.3 = (f32[1024]{0:T(1024)S(1)}, f32[1024]{0:T(1024)}, u32[]{:S(2)}) copy-start(f32[1024]{0:T(1024)} %param.13) | copy-start | bytes 12292
  26.2 20.2 %copy-start.4 = (f32[12,8]{0,1:T(8,128)S(1)}, f32[12,8]{0,1:T(8,128)}, u32[]{:S(2)}) copy-start(f32[12,8]{0,1:T(8,128)} %param.14) | copy-start | bytes 1156
  26.9 16.5 %all-to-all-start = ((bf16[3,8,6,8,128]{4,3,2,0,1:T(8,128)(2,1)}), bf16[3,8,6,8,128]{4,3,2,0,1:T(8,128)(2,1)S(1)}, u32[]{:S(2)}, u32[]{:S(2)}) async-start(bf16[3,8,6,8,128]{4,3,2,0,1:T(8,128)(2,1)} %copy.29), calls=%async_computation | async-start | bytes 589824 | tf_op jit(solution)/shard_map/all_to_all | solution.py:29
  67.7 17.2 %copy-start.2 = (f32[4096]{0:T(1024)S(1)}, f32[4096]{0:T(1024)}, u32[]{:S(2)}) copy-start(f32[4096]{0:T(1024)} %param.11) | copy-start | bytes 49156
  67.7 13.6 %collective-permute-start.2 = (bf16[1,8,6,12,128]{4,3,2,0,1:T(8,128)(2,1)S(1)}, bf16[1,8,6,12,128]{4,3,2,0,1:T(8,128)(2,1)S(1)}, u32[]{:S(2)}, u32[]{:S(2)}) collective-permute-start(bf16[1,8,6,12,128]{4,3,2,0,1:T(8,128)(2,1)S(1)} %get-tuple-element.5), channel_id=1, source_target_pairs={{0,8},{8,16},{16,24},{24,32},{32,40},{40,48},{48,56},{56,64},{64,7... | collective-permute-start | bytes 442376 | tf_op jit(solution)/shard_map/ppermute | solution.py:15
  69.6 12.1 %collective-permute-start.3 = (bf16[1,8,6,12,128]{4,3,2,0,1:T(8,128)(2,1)S(1)}, bf16[1,8,6,12,128]{4,3,2,0,1:T(8,128)(2,1)S(1)}, u32[]{:S(2)}, u32[]{:S(2)}) collective-permute-start(bf16[1,8,6,12,128]{4,3,2,0,1:T(8,128)(2,1)S(1)} %get-tuple-element.6), channel_id=1, source_target_pairs={{8,0},{16,8},{24,16},{32,24},{40,32},{48,40},{56,48},{64,56},{72,6... | collective-permute-start | bytes 442376 | tf_op jit(solution)/shard_map/ppermute | solution.py:18
where the time goes:
time: 203 us; the launch traced here: 202 us
  blocking collectives  129 us (64%)
  starting transfers between devices  34.1 us (17%)
  local copies, waits for them, and re-layouts  13.6 us (7%)
  waiting for transfers between devices  13.3 us (7%)
  matrix products  5.8 us (3%)
  other arithmetic  4.65 us (2%)
    psum x1, blocking collectives, shards(): atm_total, ocean_total = lax.psum((atm_part, ocean_part), ('grp', 'sub'))  114 us
    ppermute x2, starting transfers between devices, extended(): lax.ppermute(lax.slice_in_dim(block, 0, width, axis=dim), axis, backward)  23.4 us
    all_to_all x1, blocking collectives, flux_within(): lax.all_to_all(partial_value, 'sub', split_axis=1, concat_axis=1, tiled=T...  15.2 us
    all_to_all x1, waiting for transfers between devices, state_within(): lax.all_to_all(routed, 'sub', split_axis=1, concat_axis=1, tiled=True)  8.03 us
    all_to_all x1, starting transfers between devices, state_within(): lax.all_to_all(routed, 'sub', split_axis=1, concat_axis=1, tiled=True)  6.82 us
    ppermute x2, waiting for transfers between devices, extended(): lax.ppermute(lax.slice_in_dim(block, block.shape[dim] - width, None, axis...  4.78 us
  transfers between devices with their start and end apart: 5, of which 3 were waited for; matrix products, arithmetic and copies ran while one was open for 2% of the time, Pallas kernels for 0%

commit v1 on v0

v1 whole, which is shorter than its diff:
```python
import functools
import math

import jax
import jax.numpy as jnp
from jax import lax
from jax.experimental import pallas as pl
from jax.experimental.pallas import tpu as pltpu
from jax.sharding import PartitionSpec as P

F32 = jnp.float32
BF16 = jnp.bfloat16
VMEM = pl.BlockSpec(memory_space=pltpu.VMEM)
SMEM = pl.BlockSpec(memory_space=pltpu.SMEM)
ANY = pl.BlockSpec(memory_space=pl.ANY)
LIMIT = 48 * 1024 * 1024


def gather_kernel(block_ref, state_ref, area_ref, out_ref, fields, high, low, rows):
    subs, offsets = out_ref.shape[0], out_ref.shape[1] // 64
    blocks = area_ref.shape[0]
    for b in range(blocks):
        fields[b] = state_ref[:, b * 128 : (b + 1) * 128].astype(F32)
    upper = area_ref[...].astype(BF16).astype(F32)
    high[...] = upper
    low[...] = area_ref[...] - upper
    rows[...] = jnp.zeros_like(rows)
    for o in range(offsets):
        for k in range(subs):
            for c in range(6):
                b = block_ref[o * 6 + c, 0, k]
                rows[o * subs + k, c : c + 1, :] = high[pl.ds(b, 1), :]
                rows[o * subs + k, 8 + c : 9 + c, :] = low[pl.ds(b, 1), :]
            for c in range(0, 6, 2):
                pair = [fields[block_ref[o * 6 + c + i, 0, k]] for i in range(2)]
                out_ref[k, o * 64 + c * 8 : o * 64 + c * 8 + 16, :] = jnp.concatenate(
                    pair, axis=0
                ).astype(BF16)
            out_ref[k, o * 64 + 48 : o * 64 + 64, :] = rows[o * subs + k].astype(BF16)


def middle_kernel(
    slot_ref,
    count_ref,
    own_ref,
    before_ref,
    after_ref,
    flux_ref,
    area_ref,
    coupling_ref,
    weight_hbm,
    state_out,
    before_out,
    own_out,
    after_out,
    total_out,
    weight,
    arrived,
    taken,
    state_sum,
    acc_low,
    acc_high,
    sems,
):
    blocks, links = weight_hbm.shape[0], weight_hbm.shape[1]
    subs = own_ref.shape[0]
    copies = [
        pltpu.make_async_copy(weight_hbm.at[a], weight.at[a], sems.at[a]) for a in range(blocks)
    ]
    for copy in copies:
        copy.start()
    for p, ref in enumerate((before_ref, own_ref, after_ref)):
        for j in range(subs):
            if p == 1:
                part = ref[j, 64:128, :]
            else:
                part = ref[j]
            arrived[(p * subs + j) * 8 : (p * subs + j + 1) * 8] = part.astype(F32).reshape(8, 8, 128)
    acc_low[...] = jnp.zeros_like(acc_low)
    acc_high[...] = jnp.zeros_like(acc_high)
    for a in range(blocks):
        live = count_ref[a]
        for link in range(links):
            slot = slot_ref[a, link]
            chunk = (slot * 171) >> 10
            tile = arrived[chunk * 2 + slot]
            taken[a, :, link * 128 : (link + 1) * 128] = jnp.where(link < live, tile, 0.0)
    for a in range(blocks):
        copies[a].wait()
        state_sum[:, a * 128 : (a + 1) * 128] = jnp.dot(
            taken[a].astype(BF16),
            weight[a].reshape(links * 128, 128),
            preferred_element_type=F32,
        )
    state = state_sum[...]
    state_out[...] = state.astype(BF16)
    flux = flux_ref[...].astype(F32)
    coupling = coupling_ref[...]
    sum_low, sum_high = flux[0:8], flux[8:12]
    for f in range(state.shape[0]):
        row = state[f : f + 1, :]
        sum_low = sum_low + coupling[0:8, f : f + 1] * row
        sum_high = sum_high + coupling[8:12, f : f + 1] * row
    coupled = jnp.concatenate([sum_low, sum_high, sum_high], axis=0).astype(BF16)
    coupled_wide = coupled.astype(F32)
    half = lax.broadcasted_iota(jnp.int32, (8, 128), 0) // 4
    total_low = jnp.zeros((8, 128), F32)
    total_high = jnp.zeros((8, 128), F32)
    for a in range(blocks):
        area = area_ref[a : a + 1, :]
        total_low = total_low + coupled_wide[0:8, a * 128 : (a + 1) * 128] * area
        total_high = total_high + coupled_wide[8:16, a * 128 : (a + 1) * 128] * area
    total_high = jnp.where(half == 0, total_high, 0.0)
    for a in range(blocks):
        live = count_ref[a]
        part = lax.dot_general(
            coupled[:, a * 128 : (a + 1) * 128],
            weight[a].reshape(links * 128, 128),
            (((1,), (1,)), ((), ())),
            preferred_element_type=F32,
        )
        for link in range(links):
            slot = jnp.where(link < live, slot_ref[a, link], 6 * 3 * subs)
            columns = slice(link * 128, (link + 1) * 128)
            acc_low[slot] += part[0:8, columns]
            acc_high[slot >> 1] += jnp.where(half == (slot & 1), part[8:16, columns], 0.0)
    for p, ref in enumerate((before_out, own_out, after_out)):
        for j in range(subs):
            chunk = p * subs + j
            tiles = [acc_low[chunk * 6 + c] for c in range(6)]
            tiles = tiles + [acc_high[chunk * 3 + c] for c in range(3)]
            packed = jnp.concatenate(tiles, axis=0).astype(BF16)
            ref[j] = packed
            rounded = packed.astype(F32)
            area = arrived[chunk * 8 + 6] + arrived[chunk * 8 + 7]
            for c in range(6):
                total_low = total_low - rounded[c * 8 : c * 8 + 8] * area[c : c + 1]
            for c in range(3):
                both = jnp.where(half == 0, area[2 * c : 2 * c + 1], area[2 * c + 1 : 2 * c + 2])
                total_high = total_high - rounded[48 + c * 8 : 56 + c * 8] * both
    lane = lax.broadcasted_iota(jnp.int32, (8, 128), 1)
    field = lax.broadcasted_iota(jnp.int32, (8, 128), 0)
    low = jnp.where(lane == field, jnp.sum(total_low, axis=1, keepdims=True), 0.0)
    high = jnp.where(lane == 8 + field % 4, jnp.sum(total_high, axis=1, keepdims=True), 0.0)
    row = jnp.sum(low + high, axis=0, keepdims=True)
    total_out[...] = jnp.broadcast_to(row, total_out.shape)


def pack_kernel(total_ref, back_ref, own_ref, ahead_ref, out_ref):
    total = jnp.sum(total_ref[...], axis=0, keepdims=True)
    first = total.astype(BF16).astype(F32)
    second = (total - first).astype(BF16).astype(F32)
    third = total - first - second
    tail = jnp.concatenate([first, second, third, jnp.zeros((5, 128), F32)], axis=0)
    for j in range(out_ref.shape[0]):
        parts = [ref[j].astype(F32) for ref in (back_ref, own_ref, ahead_ref)] + [tail]
        out_ref[j] = jnp.concatenate(parts, axis=0).astype(BF16)


def final_kernel(scale, block_ref, count_ref, in_ref, flux_out, imbalance_out, low, high):
    subs = in_ref.shape[0]
    blocks = flux_out.shape[1] // 128
    low[...] = jnp.zeros_like(low)
    high[...] = jnp.zeros_like(high)
    half = lax.broadcasted_iota(jnp.int32, (8, 128), 0) // 4
    total = jnp.zeros((8, 128), F32)
    for k in range(subs):
        part = in_ref[k].astype(F32)
        for o in range(3):
            live = count_ref[o, 0, k]
            for c in range(6):
                b = jnp.where(c < live, block_ref[o * 6 + c, 0, k], blocks)
                low[b] += part[o * 72 + c * 8 : o * 72 + c * 8 + 8]
                start = o * 72 + 48 + (c // 2) * 8
                high[b] += jnp.where(half == c % 2, part[start : start + 8], 0.0)
        total = total + part[216:224]
    for b in range(blocks):
        upper = high[b]
        tile = jnp.concatenate([low[b], upper[0:4] + upper[4:8]], axis=0)
        flux_out[:, b * 128 : (b + 1) * 128] = tile.astype(BF16)
    row = jnp.sum(total, axis=0, keepdims=True) * scale
    imbalance_out[...] = row[:, : imbalance_out.shape[1]]


def shards(
    ocean_state,
    ocean_area,
    atm_flux,
    atm_area,
    coupling,
    remap_weight,
    send_block,
    send_count,
    link_slot,
    link_count,
):
    atm_blocks, links, width = remap_weight.shape[:3]
    ocean_blocks = ocean_state.shape[1] // width
    groups, subs = lax.axis_size("grp"), lax.axis_size("sub")
    forward = [(i, (i + 1) % groups) for i in range(groups)]
    backward = [(target, source) for source, target in forward]
    params = pltpu.CompilerParams(vmem_limit_bytes=LIMIT)
    chosen = send_block.transpose(1, 3, 0, 2).reshape(18, 1, subs)
    counts = send_count.transpose(1, 0, 2)

    routed = pl.pallas_call(
        gather_kernel,
        out_shape=jax.ShapeDtypeStruct((subs, 192, width), BF16),
        in_specs=[SMEM, VMEM, VMEM],
        out_specs=VMEM,
        scratch_shapes=[
            pltpu.VMEM((ocean_blocks, 8, width), F32),
            pltpu.VMEM((ocean_blocks, width), F32),
            pltpu.VMEM((ocean_blocks, width), F32),
            pltpu.VMEM((3 * subs, 16, width), F32),
        ],
        compiler_params=params,
        name="gather_slots",
    )(chosen, ocean_state, ocean_area.reshape(ocean_blocks, width))

    within = lax.all_to_all(routed, "sub", 0, 0, tiled=True)
    after = lax.ppermute(within[:, 0:64], "grp", backward)
    before = lax.ppermute(within[:, 128:192], "grp", forward)

    slots = 18 * subs
    part = jax.ShapeDtypeStruct((subs, 72, width), BF16)
    state_on_atm, part_before, part_own, part_after, totals = pl.pallas_call(
        middle_kernel,
        out_shape=(
            jax.ShapeDtypeStruct((8, atm_blocks * width), BF16),
            part,
            part,
            part,
            jax.ShapeDtypeStruct((groups, width), F32),
        ),
        in_specs=[SMEM, SMEM, VMEM, VMEM, VMEM, VMEM, VMEM, VMEM, ANY],
        out_specs=(VMEM,) * 5,
        scratch_shapes=[
            pltpu.VMEM(remap_weight.shape, BF16),
            pltpu.VMEM((24 * subs, 8, width), F32),
            pltpu.VMEM((atm_blocks, 8, links * width), F32),
            pltpu.VMEM((8, atm_blocks * width), F32),
            pltpu.VMEM((slots + 2, 8, width), F32),
            pltpu.VMEM((slots // 2 + 1, 8, width), F32),
            pltpu.SemaphoreType.DMA((atm_blocks,)),
        ],
        compiler_params=params,
        name="remap_both_ways",
    )(
        link_slot,
        link_count,
        within,
        before,
        after,
        atm_flux,
        atm_area.reshape(atm_blocks, width),
        coupling,
        remap_weight,
    )

    spread = lax.all_to_all(totals, "grp", 0, 0, tiled=True)
    back_after = lax.ppermute(part_before, "grp", backward)
    back_before = lax.ppermute(part_after, "grp", forward)

    packed = pl.pallas_call(
        pack_kernel,
        out_shape=jax.ShapeDtypeStruct((subs, 224, width), BF16),
        in_specs=[VMEM] * 4,
        out_specs=VMEM,
        compiler_params=params,
        name="pack_flux",
    )(spread, back_before, part_own, back_after)
    returned = lax.all_to_all(packed, "sub", 0, 0, tiled=True)

    scale = 1.0 / math.sqrt(groups * subs * atm_blocks * width)
    flux_on_ocean, imbalance = pl.pallas_call(
        functools.partial(final_kernel, scale),
        out_shape=(
            jax.ShapeDtypeStruct((12, ocean_blocks * width), BF16),
            jax.ShapeDtypeStruct((1, 12), F32),
        ),
        in_specs=[SMEM, SMEM, VMEM],
        out_specs=(VMEM, VMEM),
        scratch_shapes=[
            pltpu.VMEM((ocean_blocks + 1, 8, width), F32),
            pltpu.VMEM((ocean_blocks + 1, 8, width), F32),
        ],
        compiler_params=params,
        name="collect_flux",
    )(chosen, counts, returned)
    return (state_on_atm, flux_on_ocean, imbalance.reshape(12))


def solution(mesh):
    placed = (
        P(None, ("grp", "sub")),
        P(("grp", "sub")),
        P(None, ("grp", "sub")),
        P(("grp", "sub")),
        P(),
        P(("grp", "sub"), None, None, None),
        P(("grp", "sub"), None, None, None),
        P(("grp", "sub"), None, None),
        P(("grp", "sub"), None),
        P(("grp", "sub")),
    )
    return jax.shard_map(
        shards,
        mesh=mesh,
        in_specs=placed,
        out_specs=(P(None, ("grp", "sub")), P(None, ("grp", "sub")), P()),
        check_vma=False,
    )
```

time: 203 us -> 107 us (0.53)
  blocking collectives: 129 us -> 56.9 us
  starting transfers between devices: 34.1 us -> 21.3 us
  Pallas kernels: 0 us -> 8.73 us
  local copies, waits for them, and re-layouts: 13.6 us -> 7.72 us
  matrix products: 5.8 us -> 0 us
  other arithmetic: 4.65 us -> 0 us
  waiting for transfers between devices: 13.3 us -> 10.9 us
    psum x1 -> x0, blocking collectives: 114 us -> none  [shards(): atm_total, ocean_total = lax.psum((atm_part, ocean_part), ('grp', 'sub'))]
    all_to_all x1 -> x3, blocking collectives: 15.2 us -> 56.9 us  [the longest x1 21.9 us: shards(): spread = lax.all_to_all(totals, 'grp', 0, 0, tiled=True)]
    pallas_call x0 -> x4, Pallas kernels: none -> 8.73 us  [the longest x1 5.62 us: shards(): pl.pallas_call(middle_kernel, out_shape=(jax.ShapeDtypeStruct((8, atm_blo...]
    all_to_all x1 -> x0, waiting for transfers between devices: 8.03 us -> none  [state_within(): lax.all_to_all(routed, 'sub', split_axis=1, concat_axis=1, tiled=True)]
    all_to_all x1 -> x0, starting transfers between devices: 6.82 us -> none  [state_within(): lax.all_to_all(routed, 'sub', split_axis=1, concat_axis=1, tiled=True)]
    reshape x5 -> x0, local copies, waits for them, and re-layouts: 6.78 us -> none  [the longest x2 3.26 us: shards(): slot_part = slot_part.reshape(3, route_subs, capacity, fields_atm, width)]
    unnamed x14 -> x21, local copies, waits for them, and re-layouts: 1.61 us -> 7.7 us
    ppermute x4, starting transfers between devices: 27.3 us -> 21.3 us  [the longest x1 8.74 us: shards(): back_after = lax.ppermute(part_before, 'grp', backward)]
  transfers between devices with their start and end apart: 5 -> 4, of which waited for: 3 -> 1; matrix products, arithmetic and copies ran while one was open for 2% -> 1% of each run, Pallas kernels for 0% -> 0%
where the time goes in v1:
time: 107 us; the launch traced here: 106 us
  blocking collectives  56.9 us (53%)
  starting transfers between devices  21.3 us (20%)
  waiting for transfers between devices  10.9 us (10%)
  Pallas kernels  8.73 us (8%)
  local copies, waits for them, and re-layouts  7.72 us (7%)
    all_to_all x1, blocking collectives, shards(): spread = lax.all_to_all(totals, 'grp', 0, 0, tiled=True)  21.9 us
    all_to_all x1, blocking collectives, shards(): within = lax.all_to_all(routed, 'sub', 0, 0, tiled=True)  18.3 us
    all_to_all x1, blocking collectives, shards(): returned = lax.all_to_all(packed, 'sub', 0, 0, tiled=True)  16.7 us
    ppermute x1, waiting for transfers between devices, shards(): before = lax.ppermute(within[:, 128:192], 'grp', forward)  10.9 us
    ppermute x1, starting transfers between devices, shards(): back_after = lax.ppermute(part_before, 'grp', backward)  8.74 us
    ppermute x1, starting transfers between devices, shards(): after = lax.ppermute(within[:, 0:64], 'grp', backward)  8.41 us
    unnamed x21, local copies, waits for them, and re-layouts  7.7 us
    pallas_call x1, Pallas kernels, shards(): pl.pallas_call(middle_kernel, out_shape=(jax.ShapeDtypeStruct((8, atm_blo...  5.62 us
  transfers between devices with their start and end apart: 4, of which 1 were waited for; matrix products, arithmetic and copies ran while one was open for 1% of the time, Pallas kernels for 0%

profile of v1, /device:TPU:1, one launch (start us, length us, event | category | flops | bytes accessed | tf_op | source)
XLA Modules:
  0.0 106.2 jit_solution(8415047621109107541)
XLA Ops:
  0.6 0.8 copy-done.1
  1.5 0.7 copy-done.2
  2.2 0.7 copy-done.5
  2.9 1.0 gather_slots.1
  3.9 18.3 %all_to_all.21.own_ref = bf16[8,192,128]{2,1,0:T(8,128)(2,1)S(1)} all-to-all(bf16[8,192,128]{2,1,0:T(8,128)(2,1)S(1)} %gather_slots.1), channel_id=1, replica_groups=mesh['grp'=96,'sub'=8] {'sub'}, dimensions={0} | all-to-all | bytes 786432 | tf_op jit(solution)/shard_map/all_to_all | solution.py:221
  22.2 8.4 %collective-permute-start.1 = (bf16[8,64,128]{2,1,0:T(8,128)(2,1)S(1)}, bf16[8,64,128]{2,1,0:T(8,128)(2,1)S(1)}, u32[]{:S(2)}, u32[]{:S(2)}) collective-permute-start(bf16[8,64,128]{2,1,0:T(8,128)(2,1)S(1)} %get-tuple-element.17), channel_id=1, source_target_pairs={{8,0},{16,8},{24,16},{32,24},{40,32},{48,40},{56,48},{64,56},{72,6... | collective-permute-start | bytes 393224 | tf_op jit(solution)/shard_map/ppermute | solution.py:222
  30.6 2.2 %collective-permute-start = (bf16[8,64,128]{2,1,0:T(8,128)(2,1)S(1)}, bf16[8,64,128]{2,1,0:T(8,128)(2,1)S(1)}, u32[]{:S(2)}, u32[]{:S(2)}) collective-permute-start(bf16[8,64,128]{2,1,0:T(8,128)(2,1)S(1)} %get-tuple-element.18), channel_id=1, source_target_pairs={{0,8},{8,16},{16,24},{24,32},{32,40},{40,48},{48,56},{56,64},{64,7... | collective-permute-start | bytes 393224 | tf_op jit(solution)/shard_map/ppermute | solution.py:223
  32.8 0.8 copy.14.coupling_ref
  33.6 0.0 collective-permute-done.1.after_ref
  33.6 10.9 %collective-permute-done.before_ref = bf16[8,64,128]{2,1,0:T(8,128)(2,1)S(1)} collective-permute-done((bf16[8,64,128]{2,1,0:T(8,128)(2,1)S(1)}, bf16[8,64,128]{2,1,0:T(8,128)(2,1)S(1)}, u32[]{:S(2)}, u32[]{:S(2)}) %collective-permute-start) | collective-permute-done | bytes 131104 | tf_op jit(solution)/shard_map/ppermute | solution.py:223
  44.5 1.9 %copy-done = bf16[8,12,128,128]{3,2,1,0:T(8,128)(2,1)S(1)} copy-done((bf16[8,12,128,128]{3,2,1,0:T(8,128)(2,1)S(1)}, bf16[8,12,128,128]{3,2,1,0:T(8,128)(2,1)}, u32[]{:S(2)}) %copy-start) | copy-done | bytes 3145752
  46.4 0.8 copy-done.4
  47.2 0.7 copy-done.6
  47.9 0.7 copy-done.7
  48.5 0.7 copy-done.9
  49.2 5.6 %remap_both_ways.1 = (bf16[8,1024]{1,0:T(8,128)(2,1)}, bf16[8,72,128]{2,1,0:T(8,128)(2,1)S(1)}, bf16[8,72,128]{2,1,0:T(8,128)(2,1)S(1)}, bf16[8,72,128]{2,1,0:T(8,128)(2,1)S(1)}, f32[96,128]{1,0:T(8,128)S(1)}) custom-call(s32[8,12]{1,0:T(8,128)S(1)} %copy-done.6, s32[8]{0:T(128)S(1)} %copy-done.9, bf16[8,192,128]{2,1,0:T(8,128)(2,1)S(1)} %all_to_all.21.own_ref, ...), custom_call_target="tpu_custom_call" | custom-call | tf_op jit(solution)/shard_map/remap_both_ways/pallas_call | solution.py:227
  54.8 1.9 %collective-permute-start.2 = (bf16[8,72,128]{2,1,0:T(8,128)(2,1)S(1)}, bf16[8,72,128]{2,1,0:T(8,128)(2,1)S(1)}, u32[]{:S(2)}, u32[]{:S(2)}) collective-permute-start(bf16[8,72,128]{2,1,0:T(8,128)(2,1)S(1)} %get-tuple-element.12), channel_id=1, source_target_pairs={{0,8},{8,16},{16,24},{24,32},{32,40},{40,48},{48,56},{56,64},{64,7... | collective-permute-start | bytes 442376 | tf_op jit(solution)/shard_map/ppermute | solution.py:263
  56.8 8.7 %collective-permute-start.3 = (bf16[8,72,128]{2,1,0:T(8,128)(2,1)S(1)}, bf16[8,72,128]{2,1,0:T(8,128)(2,1)S(1)}, u32[]{:S(2)}, u32[]{:S(2)}) collective-permute-start(bf16[8,72,128]{2,1,0:T(8,128)(2,1)S(1)} %get-tuple-element.14), channel_id=1, source_target_pairs={{8,0},{16,8},{24,16},{32,24},{40,32},{48,40},{56,48},{64,56},{72,6... | collective-permute-start | bytes 442376 | tf_op jit(solution)/shard_map/ppermute | solution.py:262
  65.5 21.9 %all_to_all.22 = f32[96,1,128]{2,1,0:T(1,128)S(1)} all-to-all(f32[96,1,128]{2,1,0:T(1,128)S(1)} %bitcast.12), channel_id=1, replica_groups=mesh['grp'=96,'sub'=8] {'grp'}, dimensions={0} | all-to-all | bytes 98304 | tf_op jit(solution)/shard_map/all_to_all | solution.py:261
  87.4 0.0 collective-permute-done.2.back_ref
  87.4 0.0 collective-permute-done.3.ahead_ref
  87.4 0.1 pack_flux.1
  87.5 16.7 %all_to_all.23.in_ref = bf16[8,224,128]{2,1,0:T(8,128)(2,1)S(1)} all-to-all(bf16[8,224,128]{2,1,0:T(8,128)(2,1)S(1)} %pack_flux.1), channel_id=1, replica_groups=mesh['grp'=96,'sub'=8] {'sub'}, dimensions={0} | all-to-all | bytes 917504 | tf_op jit(solution)/shard_map/all_to_all | solution.py:273
  104.2 2.0 %collect_flux.1 = (bf16[12,4096]{1,0:T(8,128)(2,1)}, f32[1,12]{1,0:T(1,128)}) custom-call(s32[18,1,8]{2,1,0:T(1,128)S(1)} %bitcast.14, s32[3,1,8]{2,1,0:T(1,128)S(1)} %bitcast.17, bf16[8,224,128]{2,1,0:T(8,128)(2,1)S(1)} %all_to_all.23.in_ref), custom_call_target="tpu_custom_call" | custom-call | tf_op jit(solution)/shard_map/collect_flux/pallas_call | solution.py:276
  (13 shorter events, 0.0 us)
Async XLA Ops:
  0.6 0.8 copy-start.1
  1.5 0.7 copy-start.2
  2.2 0.7 copy-start.5
  22.2 82.0 %copy-start.3 = (s32[1,3,8,6]{2,0,3,1:T(1,128)S(1)}, s32[1,3,8,6]{2,0,3,1:T(1,128)}, u32[]{:S(2)}) copy-start(s32[1,3,8,6]{2,0,3,1:T(1,128)} %param.16) | copy-start | bytes 1732
  22.2 82.0 %copy-start.8 = (s32[1,3,8]{2,0,1:T(1,128)S(1)}, s32[1,3,8]{2,0,1:T(1,128)}, u32[]{:S(2)}) copy-start(s32[1,3,8]{2,0,1:T(1,128)} %param.17) | copy-start | bytes 292
  22.2 11.4 %collective-permute-start.1 = (bf16[8,64,128]{2,1,0:T(8,128)(2,1)S(1)}, bf16[8,64,128]{2,1,0:T(8,128)(2,1)S(1)}, u32[]{:S(2)}, u32[]{:S(2)}) collective-permute-start(bf16[8,64,128]{2,1,0:T(8,128)(2,1)S(1)} %get-tuple-element.17), channel_id=1, source_target_pairs={{8,0},{16,8},{24,16},{32,24},{40,32},{48,40},{56,48},{64,56},{72,6... | collective-permute-start | bytes 393224 | tf_op jit(solution)/shard_map/ppermute | solution.py:222
  30.6 13.9 %collective-permute-start = (bf16[8,64,128]{2,1,0:T(8,128)(2,1)S(1)}, bf16[8,64,128]{2,1,0:T(8,128)(2,1)S(1)}, u32[]{:S(2)}, u32[]{:S(2)}) collective-permute-start(bf16[8,64,128]{2,1,0:T(8,128)(2,1)S(1)} %get-tuple-element.18), channel_id=1, source_target_pairs={{0,8},{8,16},{16,24},{24,32},{32,40},{40,48},{48,56},{56,64},{64,7... | collective-permute-start | bytes 393224 | tf_op jit(solution)/shard_map/ppermute | solution.py:223
  44.5 1.9 %copy-start = (bf16[8,12,128,128]{3,2,1,0:T(8,128)(2,1)S(1)}, bf16[8,12,128,128]{3,2,1,0:T(8,128)(2,1)}, u32[]{:S(2)}) copy-start(bf16[8,12,128,128]{3,2,1,0:T(8,128)(2,1)} %weight_hbm.1) | copy-start | bytes 9437188
  46.4 0.8 copy-start.4
  47.2 0.7 copy-start.6
  47.9 0.7 copy-start.7
  48.5 0.7 copy-start.9
  54.8 32.6 %collective-permute-start.2 = (bf16[8,72,128]{2,1,0:T(8,128)(2,1)S(1)}, bf16[8,72,128]{2,1,0:T(8,128)(2,1)S(1)}, u32[]{:S(2)}, u32[]{:S(2)}) collective-permute-start(bf16[8,72,128]{2,1,0:T(8,128)(2,1)S(1)} %get-tuple-element.12), channel_id=1, source_target_pairs={{0,8},{8,16},{16,24},{24,32},{32,40},{40,48},{48,56},{56,64},{64,7... | collective-permute-start | bytes 442376 | tf_op jit(solution)/shard_map/ppermute | solution.py:263
  56.8 30.6 %collective-permute-start.3 = (bf16[8,72,128]{2,1,0:T(8,128)(2,1)S(1)}, bf16[8,72,128]{2,1,0:T(8,128)(2,1)S(1)}, u32[]{:S(2)}, u32[]{:S(2)}) collective-permute-start(bf16[8,72,128]{2,1,0:T(8,128)(2,1)S(1)} %get-tuple-element.14), channel_id=1, source_target_pairs={{8,0},{16,8},{24,16},{32,24},{40,32},{48,40},{56,48},{64,56},{72,6... | collective-permute-start | bytes 442376 | tf_op jit(solution)/shard_map/ppermute | solution.py:262

commit v2 on v1

v2 whole, which is shorter than its diff:
```python
import functools
import math

import jax
import jax.numpy as jnp
from jax import lax
from jax.experimental import pallas as pl
from jax.experimental.pallas import tpu as pltpu
from jax.sharding import PartitionSpec as P

F32 = jnp.float32
BF16 = jnp.bfloat16
VMEM = pl.BlockSpec(memory_space=pltpu.VMEM)
HBM = pl.BlockSpec(memory_space=pltpu.HBM)
WHOLE = pltpu.CompilerParams(vmem_limit_bytes=60 * 1024 * 1024)
PART = pltpu.CompilerParams(vmem_limit_bytes=16 * 1024 * 1024)


def gather_kernel(
    block_hbm, state_hbm, area_hbm, back_out, own_out, ahead_out, block, state, area, fields, high, low, rows, sems
):
    subs = own_out.shape[0]
    blocks = area_hbm.shape[0]
    copies = [
        pltpu.make_async_copy(source, target, sems.at[n])
        for n, (source, target) in enumerate(
            ((block_hbm, block), (state_hbm, state), (area_hbm, area))
        )
    ]
    for copy in copies:
        copy.start()
    rows[...] = jnp.zeros_like(rows)
    copies[2].wait()
    upper = area[...].astype(BF16).astype(F32)
    high[...] = upper
    low[...] = area[...] - upper
    copies[1].wait()
    for b in range(blocks):
        fields[b] = state[:, b * 128 : (b + 1) * 128].astype(F32)
    copies[0].wait()
    for o, out_ref in enumerate((back_out, own_out, ahead_out)):
        for k in range(subs):
            for c in range(6):
                b = block[o * 6 + c, 0, k]
                rows[o * subs + k, c : c + 1, :] = high[pl.ds(b, 1), :]
                rows[o * subs + k, 8 + c : 9 + c, :] = low[pl.ds(b, 1), :]
            for c in range(0, 6, 2):
                pair = [fields[block[o * 6 + c + i, 0, k]] for i in range(2)]
                out_ref[k, c * 8 : c * 8 + 16, :] = jnp.concatenate(pair, axis=0).astype(BF16)
            out_ref[k, 48:64, :] = rows[o * subs + k].astype(BF16)


def join_kernel(before_ref, own_ref, after_ref, out_ref):
    out_ref[:, 0:64, :] = before_ref[...]
    out_ref[:, 64:128, :] = own_ref[...]
    out_ref[:, 128:192, :] = after_ref[...]


def middle_kernel(
    slot_hbm,
    count_hbm,
    arrived_ref,
    flux_hbm,
    area_hbm,
    coupling_hbm,
    weight_hbm,
    state_out,
    part_out,
    slot_ref,
    count_ref,
    flux_ref,
    area_ref,
    coupling_ref,
    weight,
    arrived,
    taken,
    state_sum,
    acc_low,
    acc_high,
    weight_sems,
    sems,
):
    blocks, links = weight_hbm.shape[0], weight_hbm.shape[1]
    subs = arrived_ref.shape[0]
    small = [
        pltpu.make_async_copy(source, target, sems.at[n])
        for n, (source, target) in enumerate(
            (
                (slot_hbm, slot_ref),
                (count_hbm, count_ref),
                (flux_hbm, flux_ref),
                (area_hbm, area_ref),
                (coupling_hbm, coupling_ref),
            )
        )
    ]
    copies = [
        pltpu.make_async_copy(weight_hbm.at[a], weight.at[a], weight_sems.at[a])
        for a in range(blocks)
    ]
    for copy in small + copies:
        copy.start()
    for j in range(subs):
        part = arrived_ref[j].astype(F32).reshape(3, 8, 8, 128)
        for p in range(3):
            arrived[(p * subs + j) * 8 : (p * subs + j + 1) * 8] = part[p]
    acc_low[...] = jnp.zeros_like(acc_low)
    acc_high[...] = jnp.zeros_like(acc_high)
    for copy in small:
        copy.wait()
    for a in range(blocks):
        live = count_ref[a]
        for link in range(links):
            slot = slot_ref[a, link]
            chunk = (slot * 171) >> 10
            tile = arrived[chunk * 2 + slot]
            taken[a, :, link * 128 : (link + 1) * 128] = jnp.where(link < live, tile, 0.0)
    for a in range(blocks):
        copies[a].wait()
        state_sum[:, a * 128 : (a + 1) * 128] = jnp.dot(
            taken[a].astype(BF16),
            weight[a].reshape(links * 128, 128),
            preferred_element_type=F32,
        )
    state = state_sum[...]
    state_out[...] = state.astype(BF16)
    flux = flux_ref[...].astype(F32)
    coupling = jnp.transpose(coupling_ref[...])
    sum_low, sum_high = flux[0:8], flux[8:12]
    for f in range(state.shape[0]):
        row = state[f : f + 1, :]
        sum_low = sum_low + coupling[0:8, f : f + 1] * row
        sum_high = sum_high + coupling[8:12, f : f + 1] * row
    coupled = jnp.concatenate([sum_low, sum_high, sum_high], axis=0).astype(BF16)
    coupled_wide = coupled.astype(F32)
    half = lax.broadcasted_iota(jnp.int32, (8, 128), 0) // 4
    total_low = jnp.zeros((8, 128), F32)
    total_high = jnp.zeros((8, 128), F32)
    for a in range(blocks):
        area = area_ref[a : a + 1, :]
        total_low = total_low + coupled_wide[0:8, a * 128 : (a + 1) * 128] * area
        total_high = total_high + coupled_wide[8:16, a * 128 : (a + 1) * 128] * area
    total_high = jnp.where(half == 0, total_high, 0.0)
    for a in range(blocks):
        live = count_ref[a]
        part = lax.dot_general(
            coupled[:, a * 128 : (a + 1) * 128],
            weight[a].reshape(links * 128, 128),
            (((1,), (1,)), ((), ())),
            preferred_element_type=F32,
        )
        for link in range(links):
            slot = jnp.where(link < live, slot_ref[a, link], 6 * 3 * subs)
            columns = slice(link * 128, (link + 1) * 128)
            acc_low[slot] += part[0:8, columns]
            acc_high[slot >> 1] += jnp.where(half == (slot & 1), part[8:16, columns], 0.0)
    packed = []
    for j in range(subs):
        tiles = []
        for p in range(3):
            chunk = p * subs + j
            tiles += [acc_low[chunk * 6 + c] for c in range(6)]
            tiles += [acc_high[chunk * 3 + c] for c in range(3)]
        values = jnp.concatenate(tiles, axis=0).astype(BF16)
        packed.append(values)
        rounded = values.astype(F32)
        for p in range(3):
            chunk = p * subs + j
            area = arrived[chunk * 8 + 6] + arrived[chunk * 8 + 7]
            for c in range(6):
                start = p * 72 + c * 8
                total_low = total_low - rounded[start : start + 8] * area[c : c + 1]
            for c in range(3):
                start = p * 72 + 48 + c * 8
                both = jnp.where(half == 0, area[2 * c : 2 * c + 1], area[2 * c + 1 : 2 * c + 2])
                total_high = total_high - rounded[start : start + 8] * both
    lane = lax.broadcasted_iota(jnp.int32, (8, 128), 1)
    field = lax.broadcasted_iota(jnp.int32, (8, 128), 0)
    total = jnp.where(lane == field, jnp.sum(total_low, axis=1, keepdims=True), 0.0)
    total += jnp.where(lane == 8 + field % 4, jnp.sum(total_high, axis=1, keepdims=True), 0.0)
    total = jnp.sum(total, axis=0, keepdims=True)
    first = total.astype(BF16).astype(F32)
    second = (total - first).astype(BF16).astype(F32)
    third = total - first - second
    tail = jnp.concatenate([first, second, third, jnp.zeros((5, 128), F32)], axis=0)
    for j in range(subs):
        out = jnp.concatenate([packed[j].astype(F32), tail], axis=0)
        part_out[j] = out.astype(BF16)


def split_kernel(in_ref, back_out, own_out, ahead_out, total_out):
    total = jnp.zeros((8, 128), F32)
    for k in range(in_ref.shape[0]):
        part = in_ref[k].astype(F32)
        for p, ref in enumerate((back_out, own_out, ahead_out)):
            ref[k] = part[p * 72 : p * 72 + 72].astype(BF16)
        total = total + part[216:224]
    row = jnp.sum(total, axis=0, keepdims=True)
    total_out[...] = jnp.broadcast_to(row, total_out.shape)


def final_kernel(block_hbm, count_hbm, before_ref, own_ref, after_ref, flux_out, done_out, block, count, low, high, sems):
    subs = own_ref.shape[0]
    blocks = flux_out.shape[1] // 128
    copies = [
        pltpu.make_async_copy(block_hbm, block, sems.at[0]),
        pltpu.make_async_copy(count_hbm, count, sems.at[1]),
    ]
    for copy in copies:
        copy.start()
    low[...] = jnp.zeros_like(low)
    high[...] = jnp.zeros_like(high)
    half = lax.broadcasted_iota(jnp.int32, (8, 128), 0) // 4
    for copy in copies:
        copy.wait()
    for o, ref in enumerate((before_ref, own_ref, after_ref)):
        for k in range(subs):
            part = ref[k].astype(F32)
            live = count[o, 0, k]
            for c in range(6):
                b = jnp.where(c < live, block[o * 6 + c, 0, k], blocks)
                low[b] += part[c * 8 : c * 8 + 8]
                start = 48 + (c // 2) * 8
                high[b] += jnp.where(half == c % 2, part[start : start + 8], 0.0)
    for b in range(blocks):
        upper = high[b]
        tile = jnp.concatenate([low[b], upper[0:4] + upper[4:8]], axis=0)
        flux_out[:, b * 128 : (b + 1) * 128] = tile.astype(BF16)
    done_out[...] = half


def total_kernel(scale, spread_ref, done_ref, imbalance_out):
    row = jnp.sum(spread_ref[...], axis=0, keepdims=True) * scale
    imbalance_out[...] = row[:, : imbalance_out.shape[1]]


def shards(
    ocean_state,
    ocean_area,
    atm_flux,
    atm_area,
    coupling,
    remap_weight,
    send_block,
    send_count,
    link_slot,
    link_count,
):
    atm_blocks, links, width = remap_weight.shape[:3]
    ocean_blocks = ocean_state.shape[1] // width
    groups, subs = lax.axis_size("grp"), lax.axis_size("sub")
    forward = [(i, (i + 1) % groups) for i in range(groups)]
    backward = [(target, source) for source, target in forward]
    chosen = send_block.transpose(1, 3, 0, 2).reshape(18, 1, subs)
    counts = send_count.transpose(1, 0, 2)

    route = jax.ShapeDtypeStruct((subs, 64, width), BF16)
    to_back, own_slots, to_ahead = pl.pallas_call(
        gather_kernel,
        out_shape=(route, route, route),
        in_specs=[HBM, HBM, HBM],
        out_specs=(VMEM,) * 3,
        scratch_shapes=[
            pltpu.SMEM((18, 1, subs), jnp.int32),
            pltpu.VMEM(ocean_state.shape, BF16),
            pltpu.VMEM((ocean_blocks, width), F32),
            pltpu.VMEM((ocean_blocks, 8, width), F32),
            pltpu.VMEM((ocean_blocks, width), F32),
            pltpu.VMEM((ocean_blocks, width), F32),
            pltpu.VMEM((3 * subs, 16, width), F32),
            pltpu.SemaphoreType.DMA((3,)),
        ],
        compiler_params=WHOLE,
        name="gather_slots",
    )(chosen, ocean_state, ocean_area.reshape(ocean_blocks, width))

    after = lax.ppermute(to_back, "grp", backward)
    before = lax.ppermute(to_ahead, "grp", forward)
    joined = pl.pallas_call(
        join_kernel,
        out_shape=jax.ShapeDtypeStruct((subs, 192, width), BF16),
        in_specs=[VMEM] * 3,
        out_specs=VMEM,
        compiler_params=PART,
        name="join_routes",
    )(before, own_slots, after)
    arrived = lax.all_to_all(joined, "sub", 0, 0, tiled=True)

    slots = 18 * subs
    state_on_atm, partial = pl.pallas_call(
        middle_kernel,
        out_shape=(
            jax.ShapeDtypeStruct((8, atm_blocks * width), BF16),
            jax.ShapeDtypeStruct((subs, 224, width), BF16),
        ),
        in_specs=[HBM, HBM, VMEM, HBM, HBM, HBM, HBM],
        out_specs=(VMEM,) * 2,
        scratch_shapes=[
            pltpu.SMEM(link_slot.shape, jnp.int32),
            pltpu.SMEM(link_count.shape, jnp.int32),
            pltpu.VMEM(atm_flux.shape, BF16),
            pltpu.VMEM((atm_blocks, width), F32),
            pltpu.VMEM((8, 12), F32),
            pltpu.VMEM(remap_weight.shape, BF16),
            pltpu.VMEM((24 * subs, 8, width), F32),
            pltpu.VMEM((atm_blocks, 8, links * width), F32),
            pltpu.VMEM((8, atm_blocks * width), F32),
            pltpu.VMEM((slots + 2, 8, width), F32),
            pltpu.VMEM((slots // 2 + 1, 8, width), F32),
            pltpu.SemaphoreType.DMA((atm_blocks,)),
            pltpu.SemaphoreType.DMA((5,)),
        ],
        compiler_params=WHOLE,
        name="remap_both_ways",
    )(
        link_slot,
        link_count,
        arrived,
        atm_flux,
        atm_area.reshape(atm_blocks, width),
        coupling.T,
        remap_weight,
    )

    returned = lax.all_to_all(partial, "sub", 0, 0, tiled=True)
    route = jax.ShapeDtypeStruct((subs, 72, width), BF16)
    to_back, own_flux, to_ahead, totals = pl.pallas_call(
        split_kernel,
        out_shape=(route, route, route, jax.ShapeDtypeStruct((groups, width), F32)),
        in_specs=[VMEM],
        out_specs=(VMEM,) * 4,
        compiler_params=PART,
        name="split_routes",
    )(returned)
    spread = lax.all_to_all(totals, "grp", 0, 0, tiled=True)
    after = lax.ppermute(to_back, "grp", backward)
    before = lax.ppermute(to_ahead, "grp", forward)

    flux_on_ocean, done = pl.pallas_call(
        final_kernel,
        out_shape=(
            jax.ShapeDtypeStruct((12, ocean_blocks * width), BF16),
            jax.ShapeDtypeStruct((8, width), jnp.int32),
        ),
        in_specs=[HBM, HBM, VMEM, VMEM, VMEM],
        out_specs=(VMEM, VMEM),
        scratch_shapes=[
            pltpu.SMEM((18, 1, subs), jnp.int32),
            pltpu.SMEM((3, 1, subs), jnp.int32),
            pltpu.VMEM((ocean_blocks + 1, 8, width), F32),
            pltpu.VMEM((ocean_blocks + 1, 8, width), F32),
            pltpu.SemaphoreType.DMA((2,)),
        ],
        compiler_params=PART,
        cost_estimate=pl.CostEstimate(flops=10**6, bytes_accessed=8 * 10**6, transcendentals=0),
        name="collect_flux",
    )(chosen, counts, before, own_flux, after)
    scale = 1.0 / math.sqrt(groups * subs * atm_blocks * width)
    imbalance = pl.pallas_call(
        functools.partial(total_kernel, scale),
        out_shape=jax.ShapeDtypeStruct((1, 12), F32),
        in_specs=[VMEM, VMEM],
        out_specs=VMEM,
        compiler_params=PART,
        name="total_all",
    )(spread, done)
    return (state_on_atm, flux_on_ocean, imbalance.reshape(12))


def solution(mesh):
    placed = (
        P(None, ("grp", "sub")),
        P(("grp", "sub")),
        P(None, ("grp", "sub")),
        P(("grp", "sub")),
        P(),
        P(("grp", "sub"), None, None, None),
        P(("grp", "sub"), None, None, None),
        P(("grp", "sub"), None, None),
        P(("grp", "sub"), None),
        P(("grp", "sub")),
    )
    return jax.shard_map(
        shards,
        mesh=mesh,
        in_specs=placed,
        out_specs=(P(None, ("grp", "sub")), P(None, ("grp", "sub")), P()),
        check_vma=False,
    )
```

time: 107 us -> 101 us (0.944)
  blocking collectives: 56.9 us -> 28.6 us
  starting transfers between devices: 21.3 us -> 47.6 us
  local copies, waits for them, and re-layouts: 7.72 us -> 0.91 us
  Pallas kernels: 8.73 us -> 11.4 us
    all_to_all x3 -> x2, blocking collectives: 56.9 us -> 28.6 us  [the longest x1 14.8 us: shards(): returned = lax.all_to_all(partial, 'sub', 0, 0, tiled=True)]
    all_to_all x0 -> x1, starting transfers between devices: none -> 16.3 us  [shards(): spread = lax.all_to_all(totals, 'grp', 0, 0, tiled=True)]
    all_to_all x0 -> x1, waiting for transfers between devices: none -> 10.2 us  [shards(): spread = lax.all_to_all(totals, 'grp', 0, 0, tiled=True)]
    ppermute x4, starting transfers between devices: 21.3 us -> 31.3 us  [the longest x2 16.8 us: shards(): before = lax.ppermute(to_ahead, 'grp', forward)]
    ppermute x4, waiting for transfers between devices: 10.9 us -> 1.17 us  [the longest x2 1.17 us: shards(): after = lax.ppermute(to_back, 'grp', backward)]
    unnamed x21 -> x6, local copies, waits for them, and re-layouts: 7.7 us -> 0.91 us
    pallas_call x3 -> x5, Pallas kernels: 3.11 us -> 5.08 us  [the longest x1 1.98 us: shards(): pl.pallas_call(final_kernel, out_shape=(jax.ShapeDtypeStruct((12, ocean_b...]
  transfers between devices with their start and end apart: 4 -> 5, of which waited for: 1 -> 2; matrix products, arithmetic and copies ran while one was open for 1% -> 0% of each run, Pallas kernels for 0% -> 2%
where the time goes in v2:
time: 101 us
  starting transfers between devices  47.6 us (47%)
  blocking collectives  28.6 us (28%)
  Pallas kernels  11.4 us (11%)
  waiting for transfers between devices  11.3 us (11%)
    ppermute x2, starting transfers between devices, shards(): before = lax.ppermute(to_ahead, 'grp', forward)  16.8 us
    all_to_all x1, starting transfers between devices, shards(): spread = lax.all_to_all(totals, 'grp', 0, 0, tiled=True)  16.3 us
    all_to_all x1, blocking collectives, shards(): returned = lax.all_to_all(partial, 'sub', 0, 0, tiled=True)  14.8 us
    ppermute x2, starting transfers between devices, shards(): after = lax.ppermute(to_back, 'grp', backward)  14.5 us
    all_to_all x1, blocking collectives, shards(): arrived = lax.all_to_all(joined, 'sub', 0, 0, tiled=True)  13.8 us
    all_to_all x1, waiting for transfers between devices, shards(): spread = lax.all_to_all(totals, 'grp', 0, 0, tiled=True)  10.2 us
    pallas_call x1, Pallas kernels, shards(): pl.pallas_call(middle_kernel, out_shape=(jax.ShapeDtypeStruct((8, atm_blo...  6.34 us
  transfers between devices with their start and end apart: 5, of which 2 were waited for; matrix products, arithmetic and copies ran while one was open for 0% of the time, Pallas kernels for 2%

profile of v2, /device:TPU:1, one launch (start us, length us, event | category | flops | bytes accessed | tf_op | source)
XLA Modules:
  0.0 100.7 jit_solution(16343323524689440250)
XLA Ops:
  0.6 1.8 %gather_slots.1 = (bf16[8,64,128]{2,1,0:T(8,128)(2,1)}, bf16[8,64,128]{2,1,0:T(8,128)(2,1)}, bf16[8,64,128]{2,1,0:T(8,128)(2,1)}) custom-call(s32[18,1,8]{2,1,0:T(1,128)} %bitcast.13, bf16[8,4096]{1,0:T(8,128)(2,1)} %state_hbm.1, f32[32,128]{1,0:T(8,128)} %bitcast.16), custom_call_target="tpu_custom_call" | custom-call | tf_op jit(solution)/shard_map/gather_slots/pallas_call | solution.py:258
  2.5 5.4 %collective-permute-start = (bf16[8,64,128]{2,1,0:T(8,128)(2,1)}, bf16[8,64,128]{2,1,0:T(8,128)(2,1)S(1)}, u32[]{:S(2)}, u32[]{:S(2)}) collective-permute-start(bf16[8,64,128]{2,1,0:T(8,128)(2,1)} %get-tuple-element.14), channel_id=1, source_target_pairs={{0,8},{8,16},{16,24},{24,32},{32,40},{40,48},{48,56},{56,64},{64,7... | collective-permute-start | bytes 393224 | tf_op jit(solution)/shard_map/ppermute | solution.py:278
  7.9 9.0 %collective-permute-start.1 = (bf16[8,64,128]{2,1,0:T(8,128)(2,1)}, bf16[8,64,128]{2,1,0:T(8,128)(2,1)S(1)}, u32[]{:S(2)}, u32[]{:S(2)}) collective-permute-start(bf16[8,64,128]{2,1,0:T(8,128)(2,1)} %get-tuple-element.16), channel_id=1, source_target_pairs={{8,0},{16,8},{24,16},{32,24},{40,32},{48,40},{56,48},{64,56},{72,6... | collective-permute-start | bytes 393224 | tf_op jit(solution)/shard_map/ppermute | solution.py:277
  16.8 0.0 collective-permute-done.before_ref
  16.9 1.2 %collective-permute-done.1.after_ref = bf16[8,64,128]{2,1,0:T(8,128)(2,1)S(1)} collective-permute-done((bf16[8,64,128]{2,1,0:T(8,128)(2,1)}, bf16[8,64,128]{2,1,0:T(8,128)(2,1)S(1)}, u32[]{:S(2)}, u32[]{:S(2)}) %collective-permute-start.1) | collective-permute-done | bytes 131104 | tf_op jit(solution)/shard_map/ppermute | solution.py:277
  18.0 0.0 copy-start
  18.0 0.9 copy-done
  18.9 0.0 copy-start.1
  18.9 0.0 copy-start.2
  19.0 13.8 %all_to_all.21.arrived_ref = bf16[8,192,128]{2,1,0:T(8,128)(2,1)} all-to-all(bf16[8,192,128]{2,1,0:T(8,128)(2,1)S(1)} %join_routes.1), channel_id=1, replica_groups=mesh['grp'=96,'sub'=8] {'sub'}, dimensions={0} | all-to-all | bytes 786432 | tf_op jit(solution)/shard_map/all_to_all | solution.py:287
  32.8 6.3 %remap_both_ways.1 = (bf16[8,1024]{1,0:T(8,128)(2,1)}, bf16[8,224,128]{2,1,0:T(8,128)(2,1)}) custom-call(s32[8,12]{1,0:T(8,128)} %slot_hbm.1, s32[8]{0:T(128)} %count_hbm.1, bf16[8,192,128]{2,1,0:T(8,128)(2,1)} %all_to_all.21.arrived_ref, bf16[12,1024]{1,0:T(8,128)(2,1)} %flux_hbm.1, f32[8,128]{1,0:T(8,128)} %bitcast.17, f32[8,12]{1,0:T(8,128)} %bitcast.18, ...), custom_call_target="tpu_custom_call" | custom-call | tf_op jit(solution)/shard_map/remap_both_ways/pallas_call | solution.py:290
  39.1 14.8 %all_to_all.22.in_ref = bf16[8,224,128]{2,1,0:T(8,128)(2,1)S(1)} all-to-all(bf16[8,224,128]{2,1,0:T(8,128)(2,1)} %get-tuple-element.18), channel_id=1, replica_groups=mesh['grp'=96,'sub'=8] {'sub'}, dimensions={0} | all-to-all | bytes 917504 | tf_op jit(solution)/shard_map/all_to_all | solution.py:325
  53.9 0.7 split_routes.1
  54.6 11.4 %collective-permute-start.2 = (bf16[8,72,128]{2,1,0:T(8,128)(2,1)S(1)}, bf16[8,72,128]{2,1,0:T(8,128)(2,1)S(1)}, u32[]{:S(2)}, u32[]{:S(2)}) collective-permute-start(bf16[8,72,128]{2,1,0:T(8,128)(2,1)S(1)} %get-tuple-element.19), channel_id=1, source_target_pairs={{0,8},{8,16},{16,24},{24,32},{32,40},{40,48},{48,56},{56,64},{64,7... | collective-permute-start | bytes 442376 | tf_op jit(solution)/shard_map/ppermute | solution.py:337
  66.1 5.6 %collective-permute-start.3 = (bf16[8,72,128]{2,1,0:T(8,128)(2,1)S(1)}, bf16[8,72,128]{2,1,0:T(8,128)(2,1)S(1)}, u32[]{:S(2)}, u32[]{:S(2)}) collective-permute-start(bf16[8,72,128]{2,1,0:T(8,128)(2,1)S(1)} %get-tuple-element.21), channel_id=1, source_target_pairs={{8,0},{16,8},{24,16},{32,24},{40,32},{48,40},{56,48},{64,56},{72,6... | collective-permute-start | bytes 442376 | tf_op jit(solution)/shard_map/ppermute | solution.py:336
  71.7 16.3 %all-to-all-start.2 = ((f32[96,1,128]{2,1,0:T(1,128)}), f32[96,1,128]{2,1,0:T(1,128)S(1)}, u32[]{:S(2)}, u32[]{:S(2)}) async-start(f32[96,1,128]{2,1,0:T(1,128)} %bitcast.8), calls=%async_computation.2 | async-start | bytes 98304 | tf_op jit(solution)/shard_map/all_to_all | solution.py:335
  87.9 0.0 collective-permute-done.2.before_ref
  87.9 0.0 collective-permute-done.3.after_ref
  88.0 0.0 copy-done.1
  88.0 0.0 copy-done.2
  88.0 2.0 %collect_flux.1 = (bf16[12,4096]{1,0:T(8,128)(2,1)}, s32[8,128]{1,0:T(8,128)S(1)}) custom-call(s32[18,1,8]{2,1,0:T(1,128)S(1)} %bitcast.14, s32[3,1,8]{2,1,0:T(1,128)S(1)} %bitcast.15, bf16[8,72,128]{2,1,0:T(8,128)(2,1)S(1)} %collective-permute-done.2.before_ref, bf16[8,72,128]{2,1,0:T(8,128)(2,1)S(1)} %get-tuple-element.20.own_ref, ...), custom_call_target="tpu_custom_call" | custom-call | flops 1000000 | bytes 8000000 | tf_op jit(solution)/shard_map/collect_flux/pallas_call | solution.py:339
  90.0 10.2 %all-to-all-done.2 = f32[96,1,128]{2,1,0:T(1,128)S(1)} async-done(((f32[96,1,128]{2,1,0:T(1,128)}), f32[96,1,128]{2,1,0:T(1,128)S(1)}, u32[]{:S(2)}, u32[]{:S(2)}) %all-to-all-start.2) | async-done | bytes 49184 | tf_op jit(solution)/shard_map/all_to_all | solution.py:335
  100.1 0.5 total_all.1
  (1 shorter events, 0.0 us)
Async XLA Ops:
  2.5 14.4 %collective-permute-start = (bf16[8,64,128]{2,1,0:T(8,128)(2,1)}, bf16[8,64,128]{2,1,0:T(8,128)(2,1)S(1)}, u32[]{:S(2)}, u32[]{:S(2)}) collective-permute-start(bf16[8,64,128]{2,1,0:T(8,128)(2,1)} %get-tuple-element.14), channel_id=1, source_target_pairs={{0,8},{8,16},{16,24},{24,32},{32,40},{40,48},{48,56},{56,64},{64,7... | collective-permute-start | bytes 393224 | tf_op jit(solution)/shard_map/ppermute | solution.py:278
  7.9 10.1 %collective-permute-start.1 = (bf16[8,64,128]{2,1,0:T(8,128)(2,1)}, bf16[8,64,128]{2,1,0:T(8,128)(2,1)S(1)}, u32[]{:S(2)}, u32[]{:S(2)}) collective-permute-start(bf16[8,64,128]{2,1,0:T(8,128)(2,1)} %get-tuple-element.16), channel_id=1, source_target_pairs={{8,0},{16,8},{24,16},{32,24},{40,32},{48,40},{56,48},{64,56},{72,6... | collective-permute-start | bytes 393224 | tf_op jit(solution)/shard_map/ppermute | solution.py:277
  18.0 0.9 copy-start
  18.9 69.0 %copy-start.1 = (s32[1,3,8,6]{2,0,3,1:T(1,128)S(1)}, s32[1,3,8,6]{2,0,3,1:T(1,128)}, u32[]{:S(2)}) copy-start(s32[1,3,8,6]{2,0,3,1:T(1,128)} %param.16) | copy-start | bytes 1732
  18.9 69.0 %copy-start.2 = (s32[1,3,8]{2,0,1:T(1,128)S(1)}, s32[1,3,8]{2,0,1:T(1,128)}, u32[]{:S(2)}) copy-start(s32[1,3,8]{2,0,1:T(1,128)} %param.17) | copy-start | bytes 292
  54.6 33.3 %collective-permute-start.2 = (bf16[8,72,128]{2,1,0:T(8,128)(2,1)S(1)}, bf16[8,72,128]{2,1,0:T(8,128)(2,1)S(1)}, u32[]{:S(2)}, u32[]{:S(2)}) collective-permute-start(bf16[8,72,128]{2,1,0:T(8,128)(2,1)S(1)} %get-tuple-element.19), channel_id=1, source_target_pairs={{0,8},{8,16},{16,24},{24,32},{32,40},{40,48},{48,56},{56,64},{64,7... | collective-permute-start | bytes 442376 | tf_op jit(solution)/shard_map/ppermute | solution.py:337
  66.1 21.9 %collective-permute-start.3 = (bf16[8,72,128]{2,1,0:T(8,128)(2,1)S(1)}, bf16[8,72,128]{2,1,0:T(8,128)(2,1)S(1)}, u32[]{:S(2)}, u32[]{:S(2)}) collective-permute-start(bf16[8,72,128]{2,1,0:T(8,128)(2,1)S(1)} %get-tuple-element.21), channel_id=1, source_target_pairs={{8,0},{16,8},{24,16},{32,24},{40,32},{48,40},{56,48},{64,56},{72,6... | collective-permute-start | bytes 442376 | tf_op jit(solution)/shard_map/ppermute | solution.py:336
  71.7 28.5 %all-to-all-start.2 = ((f32[96,1,128]{2,1,0:T(1,128)}), f32[96,1,128]{2,1,0:T(1,128)S(1)}, u32[]{:S(2)}, u32[]{:S(2)}) async-start(f32[96,1,128]{2,1,0:T(1,128)} %bitcast.8), calls=%async_computation.2 | async-start | bytes 98304 | tf_op jit(solution)/shard_map/all_to_all | solution.py:335

commit v3 on v2

--- a/solution.py
+++ b/solution.py
@@ -11,15 +11,15 @@
 F32 = jnp.float32
 BF16 = jnp.bfloat16
 VMEM = pl.BlockSpec(memory_space=pltpu.VMEM)
+SMEM = pl.BlockSpec(memory_space=pltpu.SMEM)
 HBM = pl.BlockSpec(memory_space=pltpu.HBM)
 WHOLE = pltpu.CompilerParams(vmem_limit_bytes=60 * 1024 * 1024)
 PART = pltpu.CompilerParams(vmem_limit_bytes=16 * 1024 * 1024)
 
 
-def gather_kernel(
-    block_hbm, state_hbm, area_hbm, back_out, own_out, ahead_out, block, state, area, fields, high, low, rows, sems
-):
-    subs = own_out.shape[0]
+def gather_kernel(offsets, block_hbm, state_hbm, area_hbm, *refs):
+    outs, (block, state, area, fields, high, low, rows, sems) = refs[:-8], refs[-8:]
+    subs = outs[0].shape[0]
     blocks = area_hbm.shape[0]
     copies = [
         pltpu.make_async_copy(source, target, sems.at[n])
@@ -38,16 +38,16 @@
     for b in range(blocks):
         fields[b] = state[:, b * 128 : (b + 1) * 128].astype(F32)
     copies[0].wait()
-    for o, out_ref in enumerate((back_out, own_out, ahead_out)):
+    for n, (o, out_ref) in enumerate(zip(offsets, outs)):
         for k in range(subs):
             for c in range(6):
                 b = block[o * 6 + c, 0, k]
-                rows[o * subs + k, c : c + 1, :] = high[pl.ds(b, 1), :]
-                rows[o * subs + k, 8 + c : 9 + c, :] = low[pl.ds(b, 1), :]
+                rows[n * subs + k, c : c + 1, :] = high[pl.ds(b, 1), :]
+                rows[n * subs + k, 8 + c : 9 + c, :] = low[pl.ds(b, 1), :]
             for c in range(0, 6, 2):
                 pair = [fields[block[o * 6 + c + i, 0, k]] for i in range(2)]
                 out_ref[k, c * 8 : c * 8 + 16, :] = jnp.concatenate(pair, axis=0).astype(BF16)
-            out_ref[k, 48:64, :] = rows[o * subs + k].astype(BF16)
+            out_ref[k, 48:64, :] = rows[n * subs + k].astype(BF16)
 
 
 def join_kernel(before_ref, own_ref, after_ref, out_ref):
@@ -57,66 +57,33 @@
 
 
 def middle_kernel(
-    slot_hbm,
-    count_hbm,
+    slot_ref,
     arrived_ref,
-    flux_hbm,
-    area_hbm,
-    coupling_hbm,
-    weight_hbm,
+    column_ref,
+    weight,
     state_out,
     part_out,
-    slot_ref,
-    count_ref,
-    flux_ref,
-    area_ref,
-    coupling_ref,
-    weight,
     arrived,
     taken,
     state_sum,
     acc_low,
     acc_high,
-    weight_sems,
-    sems,
 ):
-    blocks, links = weight_hbm.shape[0], weight_hbm.shape[1]
+    blocks, links = weight.shape[0], weight.shape[1]
     subs = arrived_ref.shape[0]
-    small = [
-        pltpu.make_async_copy(source, target, sems.at[n])
-        for n, (source, target) in enumerate(
-            (
-                (slot_hbm, slot_ref),
-                (count_hbm, count_ref),
-                (flux_hbm, flux_ref),
-                (area_hbm, area_ref),
-                (coupling_hbm, coupling_ref),
-            )
-        )
-    ]
-    copies = [
-        pltpu.make_async_copy(weight_hbm.at[a], weight.at[a], weight_sems.at[a])
-        for a in range(blocks)
-    ]
-    for copy in small + copies:
-        copy.start()
+    acc_low[...] = jnp.zeros_like(acc_low)
+    acc_high[...] = jnp.zeros_like(acc_high)
     for j in range(subs):
         part = arrived_ref[j].astype(F32).reshape(3, 8, 8, 128)
         for p in range(3):
             arrived[(p * subs + j) * 8 : (p * subs + j + 1) * 8] = part[p]
-    acc_low[...] = jnp.zeros_like(acc_low)
-    acc_high[...] = jnp.zeros_like(acc_high)
-    for copy in small:
-        copy.wait()
     for a in range(blocks):
-        live = count_ref[a]
         for link in range(links):
             slot = slot_ref[a, link]
             chunk = (slot * 171) >> 10
             tile = arrived[chunk * 2 + slot]
-            taken[a, :, link * 128 : (link + 1) * 128] = jnp.where(link < live, tile, 0.0)
+            taken[a, :, link * 128 : (link + 1) * 128] = tile
     for a in range(blocks):
-        copies[a].wait()
         state_sum[:, a * 128 : (a + 1) * 128] = jnp.dot(
             taken[a].astype(BF16),
             weight[a].reshape(links * 128, 128),
@@ -124,8 +91,8 @@
         )
     state = state_sum[...]
     state_out[...] = state.astype(BF16)
-    flux = flux_ref[...].astype(F32)
-    coupling = jnp.transpose(coupling_ref[...])
+    flux = column_ref[0:12, 0 : blocks * 128]
+    coupling = column_ref[0:12, blocks * 128 : blocks * 128 + 128]
     sum_low, sum_high = flux[0:8], flux[8:12]
     for f in range(state.shape[0]):
         row = state[f : f + 1, :]
@@ -137,12 +104,11 @@
     total_low = jnp.zeros((8, 128), F32)
     total_high = jnp.zeros((8, 128), F32)
     for a in range(blocks):
-        area = area_ref[a : a + 1, :]
+        area = column_ref[12:13, a * 128 : (a + 1) * 128]
         total_low = total_low + coupled_wide[0:8, a * 128 : (a + 1) * 128] * area
         total_high = total_high + coupled_wide[8:16, a * 128 : (a + 1) * 128] * area
     total_high = jnp.where(half == 0, total_high, 0.0)
     for a in range(blocks):
-        live = count_ref[a]
         part = lax.dot_general(
             coupled[:, a * 128 : (a + 1) * 128],
             weight[a].reshape(links * 128, 128),
@@ -150,7 +116,7 @@
             preferred_element_type=F32,
         )
         for link in range(links):
-            slot = jnp.where(link < live, slot_ref[a, link], 6 * 3 * subs)
+            slot = slot_ref[a, link]
             columns = slice(link * 128, (link + 1) * 128)
             acc_low[slot] += part[0:8, columns]
             acc_high[slot >> 1] += jnp.where(half == (slot & 1), part[8:16, columns], 0.0)
@@ -188,13 +154,17 @@
         part_out[j] = out.astype(BF16)
 
 
-def split_kernel(in_ref, back_out, own_out, ahead_out, total_out):
-    total = jnp.zeros((8, 128), F32)
+def split_kernel(in_ref, back_out, own_out, ahead_out):
     for k in range(in_ref.shape[0]):
         part = in_ref[k].astype(F32)
         for p, ref in enumerate((back_out, own_out, ahead_out)):
             ref[k] = part[p * 72 : p * 72 + 72].astype(BF16)
-        total = total + part[216:224]
+
+
+def group_total_kernel(in_ref, total_out):
+    total = jnp.zeros((8, 128), F32)
+    for k in range(in_ref.shape[0]):
+        total = total + in_ref[k, 208:224, :].astype(F32)[8:16]
     row = jnp.sum(total, axis=0, keepdims=True)
     total_out[...] = jnp.broadcast_to(row, total_out.shape)
 
@@ -255,25 +225,30 @@
     counts = send_count.transpose(1, 0, 2)
 
     route = jax.ShapeDtypeStruct((subs, 64, width), BF16)
-    to_back, own_slots, to_ahead = pl.pallas_call(
-        gather_kernel,
-        out_shape=(route, route, route),
-        in_specs=[HBM, HBM, HBM],
-        out_specs=(VMEM,) * 3,
-        scratch_shapes=[
-            pltpu.SMEM((18, 1, subs), jnp.int32),
-            pltpu.VMEM(ocean_state.shape, BF16),
-            pltpu.VMEM((ocean_blocks, width), F32),
-            pltpu.VMEM((ocean_blocks, 8, width), F32),
-            pltpu.VMEM((ocean_blocks, width), F32),
-            pltpu.VMEM((ocean_blocks, width), F32),
-            pltpu.VMEM((3 * subs, 16, width), F32),
-            pltpu.SemaphoreType.DMA((3,)),
-        ],
-        compiler_params=WHOLE,
-        name="gather_slots",
-    )(chosen, ocean_state, ocean_area.reshape(ocean_blocks, width))
-
+
+    def gather(offsets, params):
+        return pl.pallas_call(
+            functools.partial(gather_kernel, offsets),
+            out_shape=(route,) * len(offsets),
+            in_specs=[HBM, HBM, HBM],
+            out_specs=(VMEM,) * len(offsets),
+            scratch_shapes=[
+                pltpu.SMEM((18, 1, subs), jnp.int32),
+                pltpu.VMEM(ocean_state.shape, BF16),
+                pltpu.VMEM((ocean_blocks, width), F32),
+                pltpu.VMEM((ocean_blocks, 8, width), F32),
+                pltpu.VMEM((ocean_blocks, width), F32),
+                pltpu.VMEM((ocean_blocks, width), F32),
+                pltpu.VMEM((len(offsets) * subs, 16, width), F32),
+                pltpu.SemaphoreType.DMA((3,)),
+            ],
+            compiler_params=params,
+            cost_estimate=pl.CostEstimate(flops=10**6, bytes_accessed=10**6, transcendentals=0),
+            name="gather_slots",
+        )(chosen, ocean_state, ocean_area.reshape(ocean_blocks, width))
+
+    to_back, to_ahead = gather((0, 2), WHOLE)
+    (own_slots,) = gather((1,), PART)
     after = lax.ppermute(to_back, "grp", backward)
     before = lax.ppermute(to_ahead, "grp", forward)
     joined = pl.pallas_call(
@@ -286,6 +261,16 @@
     )(before, own_slots, after)
     arrived = lax.all_to_all(joined, "sub", 0, 0, tiled=True)
 
+    live = lax.broadcasted_iota(jnp.int32, link_slot.shape, 1) < link_count[:, None]
+    weight = jnp.where(live[:, :, None, None], remap_weight, jnp.zeros((), BF16))
+    columns = jnp.concatenate(
+        [
+            jnp.concatenate([atm_flux.astype(F32), atm_area[None], jnp.zeros((3, atm_area.shape[0]), F32)], axis=0),
+            jnp.pad(coupling, ((0, 4), (0, width - coupling.shape[1]))),
+        ],
+        axis=1,
+    )
+
     slots = 18 * subs
     state_on_atm, partial = pl.pallas_call(
         middle_kernel,
@@ -293,42 +278,39 @@
             jax.ShapeDtypeStruct((8, atm_blocks * width), BF16),
             jax.ShapeDtypeStruct((subs, 224, width), BF16),
         ),
-        in_specs=[HBM, HBM, VMEM, HBM, HBM, HBM, HBM],
-        out_specs=(VMEM,) * 2,
+        in_specs=[SMEM] + [VMEM] * 3,
+        out_specs=(VMEM, VMEM),
         scratch_shapes=[
-            pltpu.SMEM(link_slot.shape, jnp.int32),
-            pltpu.SMEM(link_count.shape, jnp.int32),
-            pltpu.VMEM(atm_flux.shape, BF16),
-            pltpu.VMEM((atm_blocks, width), F32),
-            pltpu.VMEM((8, 12), F32),
-            pltpu.VMEM(remap_weight.shape, BF16),
             pltpu.VMEM((24 * subs, 8, width), F32),
             pltpu.VMEM((atm_blocks, 8, links * width), F32),
             pltpu.VMEM((8, atm_blocks * width), F32),
-            pltpu.VMEM((slots + 2, 8, width), F32),
-            pltpu.VMEM((slots // 2 + 1, 8, width), F32),
-            pltpu.SemaphoreType.DMA((atm_blocks,)),
-            pltpu.SemaphoreType.DMA((5,)),
+            pltpu.VMEM((slots, 8, width), F32),
+            pltpu.VMEM((slots // 2, 8, width), F32),
         ],
-        compiler_params=WHOLE,
+        compiler_params=PART,
         name="remap_both_ways",
     )(
         link_slot,
-        link_count,
         arrived,
-        atm_flux,
-        atm_area.reshape(atm_blocks, width),
-        coupling.T,
-        remap_weight,
+        columns,
+        weight,
     )
 
     returned = lax.all_to_all(partial, "sub", 0, 0, tiled=True)
     route = jax.ShapeDtypeStruct((subs, 72, width), BF16)
-    to_back, own_flux, to_ahead, totals = pl.pallas_call(
+    totals = pl.pallas_call(
+        group_total_kernel,
+        out_shape=jax.ShapeDtypeStruct((groups, width), F32),
+        in_specs=[VMEM],
+        out_specs=VMEM,
+        compiler_params=PART,
+        name="total_group",
+    )(returned)
+    to_back, own_flux, to_ahead = pl.pallas_call(
         split_kernel,
-        out_shape=(route, route, route, jax.ShapeDtypeStruct((groups, width), F32)),
+        out_shape=(route, route, route),
         in_specs=[VMEM],
-        out_specs=(VMEM,) * 4,
+        out_specs=(VMEM,) * 3,
         compiler_params=PART,
         name="split_routes",
     )(returned)

time: 101 us -> 97.5 us (0.965)
  blocking collectives: 28.6 us -> 13.8 us
  other arithmetic: 0 us -> 5.01 us
  local copies, waits for them, and re-layouts: 0.91 us -> 4.59 us
  waiting for transfers between devices: 11.3 us -> 14.4 us
  Pallas kernels: 11.4 us -> 9.19 us
  starting transfers between devices: 47.6 us -> 48.9 us
    all_to_all x1 -> x0, blocking collectives: 13.8 us -> none  [shards(): arrived = lax.all_to_all(joined, 'sub', 0, 0, tiled=True)]
    all_to_all x0 -> x1, waiting for transfers between devices: none -> 4.85 us  [shards(): arrived = lax.all_to_all(joined, 'sub', 0, 0, tiled=True)]
    pallas_call x1, Pallas kernels: 6.34 us -> 2.6 us  [shards(): pl.pallas_call(middle_kernel, out_shape=(jax.ShapeDtypeStruct((8, atm_blo...]
    unnamed x6 -> x15, local copies, waits for them, and re-layouts: 0.91 us -> 4.59 us
    all_to_all x0 -> x1, starting transfers between devices: none -> 3.45 us  [shards(): arrived = lax.all_to_all(joined, 'sub', 0, 0, tiled=True)]
    select_n x0 -> x1, other arithmetic: none -> 2.18 us  [shards(): jnp.where(live[:, :, None, None], remap_weight, jnp.zeros((), BF16))]
    concatenate x0 -> x1, other arithmetic: none -> 1.34 us  [shards(): jnp.concatenate([jnp.concatenate([atm_flux.astype(F32), atm_area[None], j...]
    ppermute x2, waiting for transfers between devices: 1.17 us -> 0.01 us  [shards(): after = lax.ppermute(to_back, 'grp', backward)]
  transfers between devices with their start and end apart: 5 -> 6, of which waited for: 2 -> 2; matrix products, arithmetic and copies ran while one was open for 0% -> 6% of each run, Pallas kernels for 2% -> 4%
where the time goes in v3:
time: 97.5 us; the launch traced here: 96.7 us
  starting transfers between devices  48.9 us (50%)
  waiting for transfers between devices  14.4 us (15%)
  blocking collectives  13.8 us (14%)
  Pallas kernels  9.19 us (9%)
  other arithmetic  5.01 us (5%)
  local copies, waits for them, and re-layouts  4.59 us (5%)
    ppermute x2, starting transfers between devices, shards(): before = lax.ppermute(to_ahead, 'grp', forward)  16 us
    all_to_all x1, starting transfers between devices, shards(): spread = lax.all_to_all(totals, 'grp', 0, 0, tiled=True)  15.9 us
    all_to_all x1, blocking collectives, shards(): returned = lax.all_to_all(partial, 'sub', 0, 0, tiled=True)  13.8 us
    ppermute x2, starting transfers between devices, shards(): after = lax.ppermute(to_back, 'grp', backward)  13.5 us
    all_to_all x1, waiting for transfers between devices, shards(): spread = lax.all_to_all(totals, 'grp', 0, 0, tiled=True)  9.51 us
    all_to_all x1, waiting for transfers between devices, shards(): arrived = lax.all_to_all(joined, 'sub', 0, 0, tiled=True)  4.85 us
    unnamed x15, local copies, waits for them, and re-layouts  4.59 us
    all_to_all x1, starting transfers between devices, shards(): arrived = lax.all_to_all(joined, 'sub', 0, 0, tiled=True)  3.45 us
  transfers between devices with their start and end apart: 6, of which 2 were waited for; matrix products, arithmetic and copies ran while one was open for 6% of the time, Pallas kernels for 4%

profile of v3, /device:TPU:1, one launch (start us, length us, event | category | flops | bytes accessed | tf_op | source)
XLA Modules:
  0.0 96.7 jit_solution(18240622900025135440)
XLA Ops:
  0.6 1.8 %gather_slots.2 = (bf16[8,64,128]{2,1,0:T(8,128)(2,1)}, bf16[8,64,128]{2,1,0:T(8,128)(2,1)}) custom-call(s32[18,1,8]{2,1,0:T(1,128)} %bitcast.12, bf16[8,4096]{1,0:T(8,128)(2,1)} %state_hbm.3, f32[32,128]{1,0:T(8,128)} %bitcast.15), custom_call_target="tpu_custom_call" | custom-call | flops 1000000 | bytes 1000000 | tf_op jit(solution)/shard_map/gather_slots/pallas_call | solution.py:230
  2.4 5.4 %collective-permute-start = (bf16[8,64,128]{2,1,0:T(8,128)(2,1)}, bf16[8,64,128]{2,1,0:T(8,128)(2,1)S(1)}, u32[]{:S(2)}, u32[]{:S(2)}) collective-permute-start(bf16[8,64,128]{2,1,0:T(8,128)(2,1)} %get-tuple-element.12), channel_id=1, source_target_pairs={{0,8},{8,16},{16,24},{24,32},{32,40},{40,48},{48,56},{56,64},{64,7... | collective-permute-start | bytes 393224 | tf_op jit(solution)/shard_map/ppermute | solution.py:253
  7.8 9.0 %collective-permute-start.1 = (bf16[8,64,128]{2,1,0:T(8,128)(2,1)}, bf16[8,64,128]{2,1,0:T(8,128)(2,1)S(1)}, u32[]{:S(2)}, u32[]{:S(2)}) collective-permute-start(bf16[8,64,128]{2,1,0:T(8,128)(2,1)} %get-tuple-element.13), channel_id=1, source_target_pairs={{8,0},{16,8},{24,16},{32,24},{40,32},{48,40},{56,48},{64,56},{72,6... | collective-permute-start | bytes 393224 | tf_op jit(solution)/shard_map/ppermute | solution.py:252
  16.8 0.8 copy-done.1
  17.6 0.7 copy-done.2
  18.3 0.7 copy-done.4
  19.0 0.8 gather_slots.3.own_ref
  19.9 0.8 join_routes.1
  20.6 3.5 %all-to-all-start = ((bf16[8,192,128]{2,1,0:T(8,128)(2,1)}), bf16[8,192,128]{2,1,0:T(8,128)(2,1)S(1)}, u32[]{:S(2)}, u32[]{:S(2)}) async-start(bf16[8,192,128]{2,1,0:T(8,128)(2,1)} %join_routes.1), calls=%async_computation | async-start | bytes 786432 | tf_op jit(solution)/shard_map/all_to_all | solution.py:262
  24.1 0.7 iota_compare_fusion.1
  24.8 0.8 copy.14
  25.6 0.8 convert_element_type.5
  26.4 1.3 %select_maximum_fusion.column_ref = f32[16,1152]{1,0:T(8,128)} fusion(f32[12,8]{1,0:T(8,128)S(1)} %copy.14, f32[3,1024]{1,0:T(4,128)S(1)} %broadcast_in_dim.21, f32[1,1024]{1,0:T(1,128)} %bitcast.18, f32[12,1024]{1,0:T(8,128)S(1)} %convert_element_type.5), kind=kLoop, calls=%fused_computation.1 | loop fusion | flops 92160 | bytes 139648 | tf_op jit(solution)/shard_map/concatenate | solution.py:266
  27.7 2.2 %broadcast_select_fusion.weight = bf16[8,12,128,128]{3,2,1,0:T(8,128)(2,1)S(1)} fusion(bf16[8,12,128,128]{3,2,1,0:T(8,128)(2,1)} %param.15, pred[8,12]{1,0:T(8,128)(4,1)S(1)} %iota_compare_fusion.1), kind=kLoop, calls=%fused_computation | loop fusion | flops 1572864 | bytes 6291552 | tf_op jit(solution)/shard_map/jit(_where)/select_n | solution.py:265
  29.9 4.9 %all-to-all-done.arrived_ref = bf16[8,192,128]{2,1,0:T(8,128)(2,1)S(1)} async-done(((bf16[8,192,128]{2,1,0:T(8,128)(2,1)}), bf16[8,192,128]{2,1,0:T(8,128)(2,1)S(1)}, u32[]{:S(2)}, u32[]{:S(2)}) %all-to-all-start) | async-done | bytes 393248 | tf_op jit(solution)/shard_map/all_to_all | solution.py:262
  34.8 0.9 copy-done
  35.7 2.6 %remap_both_ways.1 = (bf16[8,1024]{1,0:T(8,128)(2,1)}, bf16[8,224,128]{2,1,0:T(8,128)(2,1)S(1)}) custom-call(s32[8,12]{1,0:T(8,128)S(1)} %copy-done.5, bf16[8,192,128]{2,1,0:T(8,128)(2,1)S(1)} %all-to-all-done.arrived_ref, f32[16,1152]{1,0:T(8,128)S(1)} %copy-done, bf16[8,12,128,128]{3,2,1,0:T(8,128)(2,1)S(1)} %broadcast_select_fusion.weight), custom_call_target="tpu_custom_call" | custom-call | tf_op jit(solution)/shard_map/remap_both_ways/pallas_call | solution.py:275
  38.3 13.8 %all_to_all.21.in_ref = bf16[8,224,128]{2,1,0:T(8,128)(2,1)S(1)} all-to-all(bf16[8,224,128]{2,1,0:T(8,128)(2,1)S(1)} %get-tuple-element.15), channel_id=1, replica_groups=mesh['grp'=96,'sub'=8] {'sub'}, dimensions={0} | all-to-all | bytes 917504 | tf_op jit(solution)/shard_map/all_to_all | solution.py:299
  52.2 10.6 %collective-permute-start.2 = (bf16[8,72,128]{2,1,0:T(8,128)(2,1)S(1)}, bf16[8,72,128]{2,1,0:T(8,128)(2,1)S(1)}, u32[]{:S(2)}, u32[]{:S(2)}) collective-permute-start(bf16[8,72,128]{2,1,0:T(8,128)(2,1)S(1)} %get-tuple-element.16), channel_id=1, source_target_pairs={{0,8},{8,16},{16,24},{24,32},{32,40},{40,48},{48,56},{56,64},{64,7... | collective-permute-start | bytes 442376 | tf_op jit(solution)/shard_map/ppermute | solution.py:319
  62.8 4.5 %collective-permute-start.3 = (bf16[8,72,128]{2,1,0:T(8,128)(2,1)S(1)}, bf16[8,72,128]{2,1,0:T(8,128)(2,1)S(1)}, u32[]{:S(2)}, u32[]{:S(2)}) collective-permute-start(bf16[8,72,128]{2,1,0:T(8,128)(2,1)S(1)} %get-tuple-element.18), channel_id=1, source_target_pairs={{8,0},{16,8},{24,16},{32,24},{40,32},{48,40},{56,48},{64,56},{72,6... | collective-permute-start | bytes 442376 | tf_op jit(solution)/shard_map/ppermute | solution.py:318
  68.0 15.9 %all-to-all-start.2 = ((f32[96,1,128]{2,1,0:T(1,128)}), f32[96,1,128]{2,1,0:T(1,128)S(1)}, u32[]{:S(2)}, u32[]{:S(2)}) async-start(f32[96,1,128]{2,1,0:T(1,128)} %bitcast.7), calls=%async_computation.2 | async-start | bytes 98304 | tf_op jit(solution)/shard_map/all_to_all | solution.py:317
  84.0 0.7 copy-done.6
  84.6 2.0 %collect_flux.1 = (bf16[12,4096]{1,0:T(8,128)(2,1)}, s32[8,128]{1,0:T(8,128)S(1)}) custom-call(s32[18,1,8]{2,1,0:T(1,128)S(1)} %bitcast.14, s32[3,1,8]{2,1,0:T(1,128)S(1)} %bitcast.17, bf16[8,72,128]{2,1,0:T(8,128)(2,1)S(1)} %collective-permute-done.2.before_ref, bf16[8,72,128]{2,1,0:T(8,128)(2,1)S(1)} %get-tuple-element.17.own_ref, ...), custom_call_target="tpu_custom_call" | custom-call | flops 1000000 | bytes 8000000 | tf_op jit(solution)/shard_map/collect_flux/pallas_call | solution.py:321
  86.6 9.5 %all-to-all-done.2 = f32[96,1,128]{2,1,0:T(1,128)S(1)} async-done(((f32[96,1,128]{2,1,0:T(1,128)}), f32[96,1,128]{2,1,0:T(1,128)S(1)}, u32[]{:S(2)}, u32[]{:S(2)}) %all-to-all-start.2) | async-done | bytes 49184 | tf_op jit(solution)/shard_map/all_to_all | solution.py:317
  (17 shorter events, 1.3 us)
Async XLA Ops:
  2.4 17.4 %collective-permute-start = (bf16[8,64,128]{2,1,0:T(8,128)(2,1)}, bf16[8,64,128]{2,1,0:T(8,128)(2,1)S(1)}, u32[]{:S(2)}, u32[]{:S(2)}) collective-permute-start(bf16[8,64,128]{2,1,0:T(8,128)(2,1)} %get-tuple-element.12), channel_id=1, source_target_pairs={{0,8},{8,16},{16,24},{24,32},{32,40},{40,48},{48,56},{56,64},{64,7... | collective-permute-start | bytes 393224 | tf_op jit(solution)/shard_map/ppermute | solution.py:253
  7.8 12.0 %collective-permute-start.1 = (bf16[8,64,128]{2,1,0:T(8,128)(2,1)}, bf16[8,64,128]{2,1,0:T(8,128)(2,1)S(1)}, u32[]{:S(2)}, u32[]{:S(2)}) collective-permute-start(bf16[8,64,128]{2,1,0:T(8,128)(2,1)} %get-tuple-element.13), channel_id=1, source_target_pairs={{8,0},{16,8},{24,16},{32,24},{40,32},{48,40},{56,48},{64,56},{72,6... | collective-permute-start | bytes 393224 | tf_op jit(solution)/shard_map/ppermute | solution.py:252
  16.8 0.8 copy-start.1
  17.6 0.7 copy-start.2
  18.3 0.7 copy-start.4
  20.6 14.1 %all-to-all-start = ((bf16[8,192,128]{2,1,0:T(8,128)(2,1)}), bf16[8,192,128]{2,1,0:T(8,128)(2,1)S(1)}, u32[]{:S(2)}, u32[]{:S(2)}) async-start(bf16[8,192,128]{2,1,0:T(8,128)(2,1)} %join_routes.1), calls=%async_computation | async-start | bytes 786432 | tf_op jit(solution)/shard_map/all_to_all | solution.py:262
  27.7 7.0 %copy-start.5 = (s32[8,12]{1,0:T(8,128)S(1)}, s32[8,12]{1,0:T(8,128)}, u32[]{:S(2)}) copy-start(s32[8,12]{1,0:T(8,128)} %slot_ref.1) | copy-start | bytes 1156
  34.8 0.9 copy-start
  35.6 48.3 %copy-start.3 = (s32[1,3,8,6]{2,0,3,1:T(1,128)S(1)}, s32[1,3,8,6]{2,0,3,1:T(1,128)}, u32[]{:S(2)}) copy-start(s32[1,3,8,6]{2,0,3,1:T(1,128)} %param.16) | copy-start | bytes 1732
  52.2 31.8 %collective-permute-start.2 = (bf16[8,72,128]{2,1,0:T(8,128)(2,1)S(1)}, bf16[8,72,128]{2,1,0:T(8,128)(2,1)S(1)}, u32[]{:S(2)}, u32[]{:S(2)}) collective-permute-start(bf16[8,72,128]{2,1,0:T(8,128)(2,1)S(1)} %get-tuple-element.16), channel_id=1, source_target_pairs={{0,8},{8,16},{16,24},{24,32},{32,40},{40,48},{48,56},{56,64},{64,7... | collective-permute-start | bytes 442376 | tf_op jit(solution)/shard_map/ppermute | solution.py:319
  62.8 21.2 %collective-permute-start.3 = (bf16[8,72,128]{2,1,0:T(8,128)(2,1)S(1)}, bf16[8,72,128]{2,1,0:T(8,128)(2,1)S(1)}, u32[]{:S(2)}, u32[]{:S(2)}) collective-permute-start(bf16[8,72,128]{2,1,0:T(8,128)(2,1)S(1)} %get-tuple-element.18), channel_id=1, source_target_pairs={{8,0},{16,8},{24,16},{32,24},{40,32},{48,40},{56,48},{64,56},{72,6... | collective-permute-start | bytes 442376 | tf_op jit(solution)/shard_map/ppermute | solution.py:318
  68.0 28.2 %all-to-all-start.2 = ((f32[96,1,128]{2,1,0:T(1,128)}), f32[96,1,128]{2,1,0:T(1,128)S(1)}, u32[]{:S(2)}, u32[]{:S(2)}) async-start(f32[96,1,128]{2,1,0:T(1,128)} %bitcast.7), calls=%async_computation.2 | async-start | bytes 98304 | tf_op jit(solution)/shard_map/all_to_all | solution.py:317
  84.0 0.7 copy-start.6

commit v4 on v3

--- a/solution.py
+++ b/solution.py
@@ -166,37 +166,39 @@
     for k in range(in_ref.shape[0]):
         total = total + in_ref[k, 208:224, :].astype(F32)[8:16]
     row = jnp.sum(total, axis=0, keepdims=True)
-    total_out[...] = jnp.broadcast_to(row, total_out.shape)
-
-
-def final_kernel(block_hbm, count_hbm, before_ref, own_ref, after_ref, flux_out, done_out, block, count, low, high, sems):
-    subs = own_ref.shape[0]
-    blocks = flux_out.shape[1] // 128
-    copies = [
-        pltpu.make_async_copy(block_hbm, block, sems.at[0]),
-        pltpu.make_async_copy(count_hbm, count, sems.at[1]),
-    ]
-    for copy in copies:
-        copy.start()
+    spare = lax.broadcasted_iota(jnp.int32, total_out.shape, 0) % 2
+    total_out[...] = jnp.where(spare == 0, row, 0.0)
+
+
+def add_slots(o, ref, block, count, low, high):
+    half = lax.broadcasted_iota(jnp.int32, (8, 128), 0) // 4
+    for k in range(ref.shape[0]):
+        part = ref[k].astype(F32)
+        live = count[o, 0, k]
+        for c in range(6):
+            b = jnp.where(c < live, block[o * 6 + c, 0, k], low.shape[0] - 1)
+            low[b] += part[c * 8 : c * 8 + 8]
+            start = 48 + (c // 2) * 8
+            high[b] += jnp.where(half == c % 2, part[start : start + 8], 0.0)
+
+
+def own_kernel(block, count, own_ref, low, high):
     low[...] = jnp.zeros_like(low)
     high[...] = jnp.zeros_like(high)
-    half = lax.broadcasted_iota(jnp.int32, (8, 128), 0) // 4
-    for copy in copies:
-        copy.wait()
-    for o, ref in enumerate((before_ref, own_ref, after_ref)):
-        for k in range(subs):
-            part = ref[k].astype(F32)
-            live = count[o, 0, k]
-            for c in range(6):
-                b = jnp.where(c < live, block[o * 6 + c, 0, k], blocks)
-                low[b] += part[c * 8 : c * 8 + 8]
-                start = 48 + (c // 2) * 8
-                high[b] += jnp.where(half == c % 2, part[start : start + 8], 0.0)
+    add_slots(1, own_ref, block, count, low, high)
+
+
+def final_kernel(block, count, before_ref, after_ref, own_low, own_high, flux_out, done_out, low, high):
+    blocks = flux_out.shape[1] // 128
+    low[...] = own_low[...]
+    high[...] = own_high[...]
+    add_slots(0, before_ref, block, count, low, high)
+    add_slots(2, after_ref, block, count, low, high)
     for b in range(blocks):
         upper = high[b]
         tile = jnp.concatenate([low[b], upper[0:4] + upper[4:8]], axis=0)
         flux_out[:, b * 128 : (b + 1) * 128] = tile.astype(BF16)
-    done_out[...] = half
+    done_out[...] = jnp.zeros_like(done_out)
 
 
 def total_kernel(scale, spread_ref, done_ref, imbalance_out):
@@ -300,7 +302,7 @@
     route = jax.ShapeDtypeStruct((subs, 72, width), BF16)
     totals = pl.pallas_call(
         group_total_kernel,
-        out_shape=jax.ShapeDtypeStruct((groups, width), F32),
+        out_shape=jax.ShapeDtypeStruct((2 * groups, width), F32),
         in_specs=[VMEM],
         out_specs=VMEM,
         compiler_params=PART,
@@ -318,25 +320,32 @@
     after = lax.ppermute(to_back, "grp", backward)
     before = lax.ppermute(to_ahead, "grp", forward)
 
+    sums = jax.ShapeDtypeStruct((ocean_blocks + 1, 8, width), F32)
+    own_low, own_high = pl.pallas_call(
+        own_kernel,
+        out_shape=(sums, sums),
+        in_specs=[SMEM, SMEM, VMEM],
+        out_specs=(VMEM, VMEM),
+        compiler_params=PART,
+        cost_estimate=pl.CostEstimate(flops=10**6, bytes_accessed=8 * 10**6, transcendentals=0),
+        name="collect_own",
+    )(chosen, counts, own_flux)
     flux_on_ocean, done = pl.pallas_call(
         final_kernel,
         out_shape=(
             jax.ShapeDtypeStruct((12, ocean_blocks * width), BF16),
             jax.ShapeDtypeStruct((8, width), jnp.int32),
         ),
-        in_specs=[HBM, HBM, VMEM, VMEM, VMEM],
+        in_specs=[SMEM, SMEM, VMEM, VMEM, VMEM, VMEM],
         out_specs=(VMEM, VMEM),
         scratch_shapes=[
-            pltpu.SMEM((18, 1, subs), jnp.int32),
-            pltpu.SMEM((3, 1, subs), jnp.int32),
-            pltpu.VMEM((ocean_blocks + 1, 8, width), F32),
-            pltpu.VMEM((ocean_blocks + 1, 8, width), F32),
-            pltpu.SemaphoreType.DMA((2,)),
+            pltpu.VMEM(sums.shape, F32),
+            pltpu.VMEM(sums.shape, F32),
         ],
         compiler_params=PART,
         cost_estimate=pl.CostEstimate(flops=10**6, bytes_accessed=8 * 10**6, transcendentals=0),
         name="collect_flux",
-    )(chosen, counts, before, own_flux, after)
+    )(chosen, counts, before, after, own_low, own_high)
     scale = 1.0 / math.sqrt(groups * subs * atm_blocks * width)
     imbalance = pl.pallas_call(
         functools.partial(total_kernel, scale),

time: 97.5 us -> 93.5 us (0.959)
  waiting for transfers between devices: 14.4 us -> 9.98 us
    all_to_all x1, starting transfers between devices: 15.9 us -> 25.3 us  [shards(): spread = lax.all_to_all(totals, 'grp', 0, 0, tiled=True)]
    all_to_all x1, waiting for transfers between devices: 9.51 us -> 1.23 us  [shards(): spread = lax.all_to_all(totals, 'grp', 0, 0, tiled=True)]
    ppermute x2, starting transfers between devices: 16 us -> 8.93 us  [shards(): before = lax.ppermute(to_ahead, 'grp', forward)]
    ppermute x2, waiting for transfers between devices: 0.01 us -> 3.77 us  [shards(): after = lax.ppermute(to_back, 'grp', backward)]
    ppermute x2, starting transfers between devices: 13.5 us -> 10.9 us  [shards(): after = lax.ppermute(to_back, 'grp', backward)]
  transfers between devices with their start and end apart: 6 -> 6, of which waited for: 2 -> 4; matrix products, arithmetic and copies ran while one was open for 6% -> 6% of each run, Pallas kernels for 4% -> 4%
where the time goes in v4:
time: 93.5 us; the launch traced here: 92.7 us
  starting transfers between devices  48.5 us (52%)
  blocking collectives  13.8 us (15%)
  Pallas kernels  9.98 us (11%)
  waiting for transfers between devices  9.98 us (11%)
  other arithmetic  5 us (5%)
  local copies, waits for them, and re-layouts  4.6 us (5%)
    all_to_all x1, starting transfers between devices, shards(): spread = lax.all_to_all(totals, 'grp', 0, 0, tiled=True)  25.3 us
    all_to_all x1, blocking collectives, shards(): returned = lax.all_to_all(partial, 'sub', 0, 0, tiled=True)  13.8 us
    ppermute x2, starting transfers between devices, shards(): after = lax.ppermute(to_back, 'grp', backward)  10.9 us
    ppermute x2, starting transfers between devices, shards(): before = lax.ppermute(to_ahead, 'grp', forward)  8.93 us
    all_to_all x1, waiting for transfers between devices, shards(): arrived = lax.all_to_all(joined, 'sub', 0, 0, tiled=True)  4.87 us
    unnamed x15, local copies, waits for them, and re-layouts  4.6 us
    ppermute x2, waiting for transfers between devices, shards(): after = lax.ppermute(to_back, 'grp', backward)  3.77 us
    all_to_all x1, starting transfers between devices, shards(): arrived = lax.all_to_all(joined, 'sub', 0, 0, tiled=True)  3.45 us
  transfers between devices with their start and end apart: 6, of which 4 were waited for; matrix products, arithmetic and copies ran while one was open for 6% of the time, Pallas kernels for 4%

profile of v4, /device:TPU:1, one launch (start us, length us, event | category | flops | bytes accessed | tf_op | source)
XLA Modules:
  0.0 92.7 jit_solution(14683053644903758497)
XLA Ops:
  0.6 1.8 %gather_slots.2 = (bf16[8,64,128]{2,1,0:T(8,128)(2,1)}, bf16[8,64,128]{2,1,0:T(8,128)(2,1)}) custom-call(s32[18,1,8]{2,1,0:T(1,128)} %bitcast.10, bf16[8,4096]{1,0:T(8,128)(2,1)} %state_hbm.3, f32[32,128]{1,0:T(8,128)} %bitcast.14), custom_call_target="tpu_custom_call" | custom-call | flops 1000000 | bytes 1000000 | tf_op jit(solution)/shard_map/gather_slots/pallas_call | solution.py:232
  2.4 5.4 %collective-permute-start = (bf16[8,64,128]{2,1,0:T(8,128)(2,1)}, bf16[8,64,128]{2,1,0:T(8,128)(2,1)S(1)}, u32[]{:S(2)}, u32[]{:S(2)}) collective-permute-start(bf16[8,64,128]{2,1,0:T(8,128)(2,1)} %get-tuple-element.14), channel_id=1, source_target_pairs={{0,8},{8,16},{16,24},{24,32},{32,40},{40,48},{48,56},{56,64},{64,7... | collective-permute-start | bytes 393224 | tf_op jit(solution)/shard_map/ppermute | solution.py:255
  7.8 9.0 %collective-permute-start.1 = (bf16[8,64,128]{2,1,0:T(8,128)(2,1)}, bf16[8,64,128]{2,1,0:T(8,128)(2,1)S(1)}, u32[]{:S(2)}, u32[]{:S(2)}) collective-permute-start(bf16[8,64,128]{2,1,0:T(8,128)(2,1)} %get-tuple-element.15), channel_id=1, source_target_pairs={{8,0},{16,8},{24,16},{32,24},{40,32},{48,40},{56,48},{64,56},{72,6... | collective-permute-start | bytes 393224 | tf_op jit(solution)/shard_map/ppermute | solution.py:254
  16.8 0.8 copy-done.1
  18.3 0.7 copy-done.4
  19.0 0.8 gather_slots.3.own_ref
  19.9 0.8 join_routes.1
  20.6 3.5 %all-to-all-start = ((bf16[8,192,128]{2,1,0:T(8,128)(2,1)}), bf16[8,192,128]{2,1,0:T(8,128)(2,1)S(1)}, u32[]{:S(2)}, u32[]{:S(2)}) async-start(bf16[8,192,128]{2,1,0:T(8,128)(2,1)} %join_routes.1), calls=%async_computation | async-start | bytes 786432 | tf_op jit(solution)/shard_map/all_to_all | solution.py:264
  24.1 0.7 iota_compare_fusion.1
  24.8 0.8 copy.13
  25.6 0.8 convert_element_type.5
  26.4 1.3 %select_maximum_fusion.column_ref = f32[16,1152]{1,0:T(8,128)} fusion(f32[12,8]{1,0:T(8,128)S(1)} %copy.13, f32[3,1024]{1,0:T(4,128)S(1)} %broadcast_in_dim.21, f32[1,1024]{1,0:T(1,128)} %bitcast.18, f32[12,1024]{1,0:T(8,128)S(1)} %convert_element_type.5), kind=kLoop, calls=%fused_computation.1 | loop fusion | flops 92160 | bytes 139648 | tf_op jit(solution)/shard_map/concatenate | solution.py:268
  27.7 2.2 %broadcast_select_fusion.weight = bf16[8,12,128,128]{3,2,1,0:T(8,128)(2,1)S(1)} fusion(bf16[8,12,128,128]{3,2,1,0:T(8,128)(2,1)} %param.15, pred[8,12]{1,0:T(8,128)(4,1)S(1)} %iota_compare_fusion.1), kind=kLoop, calls=%fused_computation | loop fusion | flops 1572864 | bytes 6291552 | tf_op jit(solution)/shard_map/jit(_where)/select_n | solution.py:267
  29.9 4.9 %all-to-all-done.arrived_ref = bf16[8,192,128]{2,1,0:T(8,128)(2,1)S(1)} async-done(((bf16[8,192,128]{2,1,0:T(8,128)(2,1)}), bf16[8,192,128]{2,1,0:T(8,128)(2,1)S(1)}, u32[]{:S(2)}, u32[]{:S(2)}) %all-to-all-start) | async-done | bytes 393248 | tf_op jit(solution)/shard_map/all_to_all | solution.py:264
  34.7 0.9 copy-done
  36.3 2.6 %remap_both_ways.1 = (bf16[8,1024]{1,0:T(8,128)(2,1)}, bf16[8,224,128]{2,1,0:T(8,128)(2,1)S(1)}) custom-call(s32[8,12]{1,0:T(8,128)S(1)} %copy-done.6, bf16[8,192,128]{2,1,0:T(8,128)(2,1)S(1)} %all-to-all-done.arrived_ref, f32[16,1152]{1,0:T(8,128)S(1)} %copy-done, bf16[8,12,128,128]{3,2,1,0:T(8,128)(2,1)S(1)} %broadcast_select_fusion.weight), custom_call_target="tpu_custom_call" | custom-call | tf_op jit(solution)/shard_map/remap_both_ways/pallas_call | solution.py:277
  38.9 13.8 %all_to_all.21.in_ref = bf16[8,224,128]{2,1,0:T(8,128)(2,1)S(1)} all-to-all(bf16[8,224,128]{2,1,0:T(8,128)(2,1)S(1)} %get-tuple-element.17), channel_id=1, replica_groups=mesh['grp'=96,'sub'=8] {'sub'}, dimensions={0} | all-to-all | bytes 917504 | tf_op jit(solution)/shard_map/all_to_all | solution.py:301
  53.4 25.3 %all-to-all-start.2 = ((f32[96,2,128]{2,1,0:T(2,128)}), f32[96,2,128]{2,1,0:T(2,128)S(1)}, u32[]{:S(2)}, u32[]{:S(2)}) async-start(f32[96,2,128]{2,1,0:T(2,128)} %bitcast.6), calls=%async_computation.2 | async-start | bytes 196608 | tf_op jit(solution)/shard_map/all_to_all | solution.py:319
  78.7 3.5 %collective-permute-start.2 = (bf16[8,72,128]{2,1,0:T(8,128)(2,1)S(1)}, bf16[8,72,128]{2,1,0:T(8,128)(2,1)S(1)}, u32[]{:S(2)}, u32[]{:S(2)}) collective-permute-start(bf16[8,72,128]{2,1,0:T(8,128)(2,1)S(1)} %get-tuple-element.18), channel_id=1, source_target_pairs={{0,8},{8,16},{16,24},{24,32},{32,40},{40,48},{48,56},{56,64},{64,7... | collective-permute-start | bytes 442376 | tf_op jit(solution)/shard_map/ppermute | solution.py:321
  82.3 1.9 %collective-permute-start.3 = (bf16[8,72,128]{2,1,0:T(8,128)(2,1)S(1)}, bf16[8,72,128]{2,1,0:T(8,128)(2,1)S(1)}, u32[]{:S(2)}, u32[]{:S(2)}) collective-permute-start(bf16[8,72,128]{2,1,0:T(8,128)(2,1)S(1)} %get-tuple-element.19), channel_id=1, source_target_pairs={{8,0},{16,8},{24,16},{32,24},{40,32},{48,40},{56,48},{64,56},{72,6... | collective-permute-start | bytes 442376 | tf_op jit(solution)/shard_map/ppermute | solution.py:320
  84.2 0.9 collect_own.1
  85.3 3.8 %collective-permute-done.3.after_ref = bf16[8,72,128]{2,1,0:T(8,128)(2,1)S(1)} collective-permute-done((bf16[8,72,128]{2,1,0:T(8,128)(2,1)S(1)}, bf16[8,72,128]{2,1,0:T(8,128)(2,1)S(1)}, u32[]{:S(2)}, u32[]{:S(2)}) %collective-permute-start.3) | collective-permute-done | bytes 147488 | tf_op jit(solution)/shard_map/ppermute | solution.py:320
  89.1 1.8 %collect_flux.1 = (bf16[12,4096]{1,0:T(8,128)(2,1)}, s32[8,128]{1,0:T(8,128)S(1)}) custom-call(s32[18,1,8]{2,1,0:T(1,128)S(1)} %bitcast.13, s32[3,1,8]{2,1,0:T(1,128)S(1)} %bitcast.17, bf16[8,72,128]{2,1,0:T(8,128)(2,1)S(1)} %collective-permute-done.2.before_ref, bf16[8,72,128]{2,1,0:T(8,128)(2,1)S(1)} %collective-permute-done.3.after_ref, ...), custom_call_target="tpu_custom_call" | custom-call | flops 1000000 | bytes 8000000 | tf_op jit(solution)/shard_map/collect_flux/pallas_call | solution.py:333
  90.9 1.2 %all-to-all-done.2 = f32[96,2,128]{2,1,0:T(2,128)S(1)} async-done(((f32[96,2,128]{2,1,0:T(2,128)}), f32[96,2,128]{2,1,0:T(2,128)S(1)}, u32[]{:S(2)}, u32[]{:S(2)}) %all-to-all-start.2) | async-done | bytes 98336 | tf_op jit(solution)/shard_map/all_to_all | solution.py:319
  (18 shorter events, 2.8 us)
Async XLA Ops:
  2.4 17.4 %collective-permute-start = (bf16[8,64,128]{2,1,0:T(8,128)(2,1)}, bf16[8,64,128]{2,1,0:T(8,128)(2,1)S(1)}, u32[]{:S(2)}, u32[]{:S(2)}) collective-permute-start(bf16[8,64,128]{2,1,0:T(8,128)(2,1)} %get-tuple-element.14), channel_id=1, source_target_pairs={{0,8},{8,16},{16,24},{24,32},{32,40},{40,48},{48,56},{56,64},{64,7... | collective-permute-start | bytes 393224 | tf_op jit(solution)/shard_map/ppermute | solution.py:255
  7.8 12.0 %collective-permute-start.1 = (bf16[8,64,128]{2,1,0:T(8,128)(2,1)}, bf16[8,64,128]{2,1,0:T(8,128)(2,1)S(1)}, u32[]{:S(2)}, u32[]{:S(2)}) collective-permute-start(bf16[8,64,128]{2,1,0:T(8,128)(2,1)} %get-tuple-element.15), channel_id=1, source_target_pairs={{8,0},{16,8},{24,16},{32,24},{40,32},{48,40},{56,48},{64,56},{72,6... | collective-permute-start | bytes 393224 | tf_op jit(solution)/shard_map/ppermute | solution.py:254
  16.8 0.8 copy-start.1
  17.6 0.7 copy-start.2
  18.3 0.7 copy-start.4
  20.6 14.1 %all-to-all-start = ((bf16[8,192,128]{2,1,0:T(8,128)(2,1)}), bf16[8,192,128]{2,1,0:T(8,128)(2,1)S(1)}, u32[]{:S(2)}, u32[]{:S(2)}) async-start(bf16[8,192,128]{2,1,0:T(8,128)(2,1)} %join_routes.1), calls=%async_computation | async-start | bytes 786432 | tf_op jit(solution)/shard_map/all_to_all | solution.py:264
  34.7 0.9 copy-start
  35.6 0.7 copy-start.6
  36.3 47.9 %copy-start.3 = (s32[1,3,8,6]{2,0,3,1:T(1,128)S(1)}, s32[1,3,8,6]{2,0,3,1:T(1,128)}, u32[]{:S(2)}) copy-start(s32[1,3,8,6]{2,0,3,1:T(1,128)} %param.16) | copy-start | bytes 1732
  36.3 47.9 %copy-start.5 = (s32[1,3,8]{2,0,1:T(1,128)S(1)}, s32[1,3,8]{2,0,1:T(1,128)}, u32[]{:S(2)}) copy-start(s32[1,3,8]{2,0,1:T(1,128)} %param.17) | copy-start | bytes 292
  53.4 38.7 %all-to-all-start.2 = ((f32[96,2,128]{2,1,0:T(2,128)}), f32[96,2,128]{2,1,0:T(2,128)S(1)}, u32[]{:S(2)}, u32[]{:S(2)}) async-start(f32[96,2,128]{2,1,0:T(2,128)} %bitcast.6), calls=%async_computation.2 | async-start | bytes 196608 | tf_op jit(solution)/shard_map/all_to_all | solution.py:319
  78.7 6.5 %collective-permute-start.2 = (bf16[8,72,128]{2,1,0:T(8,128)(2,1)S(1)}, bf16[8,72,128]{2,1,0:T(8,128)(2,1)S(1)}, u32[]{:S(2)}, u32[]{:S(2)}) collective-permute-start(bf16[8,72,128]{2,1,0:T(8,128)(2,1)S(1)} %get-tuple-element.18), channel_id=1, source_target_pairs={{0,8},{8,16},{16,24},{24,32},{32,40},{40,48},{48,56},{56,64},{64,7... | collective-permute-start | bytes 442376 | tf_op jit(solution)/shard_map/ppermute | solution.py:321
  82.3 6.8 %collective-permute-start.3 = (bf16[8,72,128]{2,1,0:T(8,128)(2,1)S(1)}, bf16[8,72,128]{2,1,0:T(8,128)(2,1)S(1)}, u32[]{:S(2)}, u32[]{:S(2)}) collective-permute-start(bf16[8,72,128]{2,1,0:T(8,128)(2,1)S(1)} %get-tuple-element.19), channel_id=1, source_target_pairs={{8,0},{16,8},{24,16},{32,24},{40,32},{48,40},{56,48},{64,56},{72,6... | collective-permute-start | bytes 442376 | tf_op jit(solution)/shard_map/ppermute | solution.py:320

commit v5 on v4

--- a/solution.py
+++ b/solution.py
@@ -17,9 +17,8 @@
 PART = pltpu.CompilerParams(vmem_limit_bytes=16 * 1024 * 1024)
 
 
-def gather_kernel(offsets, block_hbm, state_hbm, area_hbm, *refs):
-    outs, (block, state, area, fields, high, low, rows, sems) = refs[:-8], refs[-8:]
-    subs = outs[0].shape[0]
+def gather_kernel(block_hbm, state_hbm, area_hbm, out_ref, block, state, area, fields, high, low, rows, sems):
+    subs = out_ref.shape[0]
     blocks = area_hbm.shape[0]
     copies = [
         pltpu.make_async_copy(source, target, sems.at[n])
@@ -38,27 +37,29 @@
     for b in range(blocks):
         fields[b] = state[:, b * 128 : (b + 1) * 128].astype(F32)
     copies[0].wait()
-    for n, (o, out_ref) in enumerate(zip(offsets, outs)):
+    for o in range(3):
         for k in range(subs):
             for c in range(6):
                 b = block[o * 6 + c, 0, k]
-                rows[n * subs + k, c : c + 1, :] = high[pl.ds(b, 1), :]
-                rows[n * subs + k, 8 + c : 9 + c, :] = low[pl.ds(b, 1), :]
+                rows[o * subs + k, c : c + 1, :] = high[pl.ds(b, 1), :]
+                rows[o * subs + k, 8 + c : 9 + c, :] = low[pl.ds(b, 1), :]
             for c in range(0, 6, 2):
                 pair = [fields[block[o * 6 + c + i, 0, k]] for i in range(2)]
-                out_ref[k, c * 8 : c * 8 + 16, :] = jnp.concatenate(pair, axis=0).astype(BF16)
-            out_ref[k, 48:64, :] = rows[n * subs + k].astype(BF16)
-
-
-def join_kernel(before_ref, own_ref, after_ref, out_ref):
-    out_ref[:, 0:64, :] = before_ref[...]
-    out_ref[:, 64:128, :] = own_ref[...]
-    out_ref[:, 128:192, :] = after_ref[...]
+                start = o * 64 + c * 8
+                out_ref[k, start : start + 16, :] = jnp.concatenate(pair, axis=0).astype(BF16)
+            out_ref[k, o * 64 + 48 : o * 64 + 64, :] = rows[o * subs + k].astype(BF16)
+
+
+def forward_kernel(in_ref, back_out, ahead_out):
+    back_out[...] = in_ref[:, 0:64, :]
+    ahead_out[...] = in_ref[:, 128:192, :]
 
 
 def middle_kernel(
     slot_ref,
-    arrived_ref,
+    within_ref,
+    before_ref,
+    after_ref,
     column_ref,
     weight,
     state_out,
@@ -70,13 +71,13 @@
     acc_high,
 ):
     blocks, links = weight.shape[0], weight.shape[1]
-    subs = arrived_ref.shape[0]
+    subs = within_ref.shape[0]
     acc_low[...] = jnp.zeros_like(acc_low)
     acc_high[...] = jnp.zeros_like(acc_high)
     for j in range(subs):
-        part = arrived_ref[j].astype(F32).reshape(3, 8, 8, 128)
-        for p in range(3):
-            arrived[(p * subs + j) * 8 : (p * subs + j + 1) * 8] = part[p]
+        for p, part in enumerate((before_ref[j], within_ref[j, 64:128, :], after_ref[j])):
+            tiles = part.astype(F32).reshape(8, 8, 128)
+            arrived[(p * subs + j) * 8 : (p * subs + j + 1) * 8] = tiles
     for a in range(blocks):
         for link in range(links):
             slot = slot_ref[a, link]
@@ -170,33 +171,35 @@
     total_out[...] = jnp.where(spare == 0, row, 0.0)
 
 
-def add_slots(o, ref, block, count, low, high):
+def add_slots(offsets, refs, block, count, lows, highs):
     half = lax.broadcasted_iota(jnp.int32, (8, 128), 0) // 4
-    for k in range(ref.shape[0]):
-        part = ref[k].astype(F32)
-        live = count[o, 0, k]
+    for k in range(refs[0].shape[0]):
+        parts = [ref[k].astype(F32) for ref in refs]
         for c in range(6):
-            b = jnp.where(c < live, block[o * 6 + c, 0, k], low.shape[0] - 1)
-            low[b] += part[c * 8 : c * 8 + 8]
-            start = 48 + (c // 2) * 8
-            high[b] += jnp.where(half == c % 2, part[start : start + 8], 0.0)
+            for o, part, low, high in zip(offsets, parts, lows, highs):
+                b = jnp.where(c < count[o, 0, k], block[o * 6 + c, 0, k], low.shape[0] - 1)
+                low[b] += part[c * 8 : c * 8 + 8]
+                start = 48 + (c // 2) * 8
+                high[b] += jnp.where(half == c % 2, part[start : start + 8], 0.0)
 
 
 def own_kernel(block, count, own_ref, low, high):
     low[...] = jnp.zeros_like(low)
     high[...] = jnp.zeros_like(high)
-    add_slots(1, own_ref, block, count, low, high)
-
-
-def final_kernel(block, count, before_ref, after_ref, own_low, own_high, flux_out, done_out, low, high):
+    add_slots((1,), (own_ref,), block, count, (low,), (high,))
+
+
+def final_kernel(block, count, before_ref, after_ref, own_low, own_high, flux_out, done_out, low, high, more_low, more_high):
     blocks = flux_out.shape[1] // 128
-    low[...] = own_low[...]
-    high[...] = own_high[...]
-    add_slots(0, before_ref, block, count, low, high)
-    add_slots(2, after_ref, block, count, low, high)
+    for ref in (low, high, more_low, more_high):
+        ref[...] = jnp.zeros_like(ref)
+    add_slots(
+        (0, 2), (before_ref, after_ref), block, count, (low, more_low), (high, more_high)
+    )
     for b in range(blocks):
-        upper = high[b]
-        tile = jnp.concatenate([low[b], upper[0:4] + upper[4:8]], axis=0)
+        upper = high[b] + more_high[b] + own_high[b]
+        lower = low[b] + more_low[b] + own_low[b]
+        tile = jnp.concatenate([lower, upper[0:4] + upper[4:8]], axis=0)
         flux_out[:, b * 128 : (b + 1) * 128] = tile.astype(BF16)
     done_out[...] = jnp.zeros_like(done_out)
 
@@ -226,42 +229,36 @@
     chosen = send_block.transpose(1, 3, 0, 2).reshape(18, 1, subs)
     counts = send_count.transpose(1, 0, 2)
 
+    routed = pl.pallas_call(
+        gather_kernel,
+        out_shape=jax.ShapeDtypeStruct((subs, 192, width), BF16),
+        in_specs=[HBM, HBM, HBM],
+        out_specs=VMEM,
+        scratch_shapes=[
+            pltpu.SMEM((18, 1, subs), jnp.int32),
+            pltpu.VMEM(ocean_state.shape, BF16),
+            pltpu.VMEM((ocean_blocks, width), F32),
+            pltpu.VMEM((ocean_blocks, 8, width), F32),
+            pltpu.VMEM((ocean_blocks, width), F32),
+            pltpu.VMEM((ocean_blocks, width), F32),
+            pltpu.VMEM((3 * subs, 16, width), F32),
+            pltpu.SemaphoreType.DMA((3,)),
+        ],
+        compiler_params=WHOLE,
+        name="gather_slots",
+    )(chosen, ocean_state, ocean_area.reshape(ocean_blocks, width))
+    within = lax.all_to_all(routed, "sub", 0, 0, tiled=True)
     route = jax.ShapeDtypeStruct((subs, 64, width), BF16)
-
-    def gather(offsets, params):
-        return pl.pallas_call(
-            functools.partial(gather_kernel, offsets),
-            out_shape=(route,) * len(offsets),
-            in_specs=[HBM, HBM, HBM],
-            out_specs=(VMEM,) * len(offsets),
-            scratch_shapes=[
-                pltpu.SMEM((18, 1, subs), jnp.int32),
-                pltpu.VMEM(ocean_state.shape, BF16),
-                pltpu.VMEM((ocean_blocks, width), F32),
-                pltpu.VMEM((ocean_blocks, 8, width), F32),
-                pltpu.VMEM((ocean_blocks, width), F32),
-                pltpu.VMEM((ocean_blocks, width), F32),
-                pltpu.VMEM((len(offsets) * subs, 16, width), F32),
-                pltpu.SemaphoreType.DMA((3,)),
-            ],
-            compiler_params=params,
-            cost_estimate=pl.CostEstimate(flops=10**6, bytes_accessed=10**6, transcendentals=0),
-            name="gather_slots",
-        )(chosen, ocean_state, ocean_area.reshape(ocean_blocks, width))
-
-    to_back, to_ahead = gather((0, 2), WHOLE)
-    (own_slots,) = gather((1,), PART)
+    to_back, to_ahead = pl.pallas_call(
+        forward_kernel,
+        out_shape=(route, route),
+        in_specs=[VMEM],
+        out_specs=(VMEM, VMEM),
+        compiler_params=PART,
+        name="forward_routes",
+    )(within)
     after = lax.ppermute(to_back, "grp", backward)
     before = lax.ppermute(to_ahead, "grp", forward)
-    joined = pl.pallas_call(
-        join_kernel,
-        out_shape=jax.ShapeDtypeStruct((subs, 192, width), BF16),
-        in_specs=[VMEM] * 3,
-        out_specs=VMEM,
-        compiler_params=PART,
-        name="join_routes",
-    )(before, own_slots, after)
-    arrived = lax.all_to_all(joined, "sub", 0, 0, tiled=True)
 
     live = lax.broadcasted_iota(jnp.int32, link_slot.shape, 1) < link_count[:, None]
     weight = jnp.where(live[:, :, None, None], remap_weight, jnp.zeros((), BF16))
@@ -280,7 +277,7 @@
             jax.ShapeDtypeStruct((8, atm_blocks * width), BF16),
             jax.ShapeDtypeStruct((subs, 224, width), BF16),
         ),
-        in_specs=[SMEM] + [VMEM] * 3,
+        in_specs=[SMEM] + [VMEM] * 5,
         out_specs=(VMEM, VMEM),
         scratch_shapes=[
             pltpu.VMEM((24 * subs, 8, width), F32),
@@ -293,7 +290,9 @@
         name="remap_both_ways",
     )(
         link_slot,
-        arrived,
+        within,
+        before,
+        after,
         columns,
         weight,
     )
@@ -341,6 +340,8 @@
         scratch_shapes=[
             pltpu.VMEM(sums.shape, F32),
             pltpu.VMEM(sums.shape, F32),
+            pltpu.VMEM(sums.shape, F32),
+            pltpu.VMEM(sums.shape, F32),
         ],
         compiler_params=PART,
         cost_estimate=pl.CostEstimate(flops=10**6, bytes_accessed=8 * 10**6, transcendentals=0),

time: 93.5 us -> 90.6 us (0.969)
  waiting for transfers between devices: 9.98 us -> 13.3 us
  local copies, waits for them, and re-layouts: 4.6 us -> 2.06 us
  starting transfers between devices: 48.5 us -> 46.3 us
  Pallas kernels: 9.98 us -> 8.44 us
    ppermute x2, starting transfers between devices: 10.9 us -> 4.34 us  [shards(): after = lax.ppermute(to_back, 'grp', backward)]
    all_to_all x1, starting transfers between devices: 3.45 us -> 7.66 us  [shards(): within = lax.all_to_all(routed, 'sub', 0, 0, tiled=True)]
    ppermute x2, starting transfers between devices: 8.93 us -> 12.3 us  [shards(): before = lax.ppermute(to_ahead, 'grp', forward)]
    all_to_all x1, starting transfers between devices: 25.3 us -> 22 us  [shards(): spread = lax.all_to_all(totals, 'grp', 0, 0, tiled=True)]
    ppermute x2, waiting for transfers between devices: 3.77 us -> 6.71 us  [shards(): after = lax.ppermute(to_back, 'grp', backward)]
    unnamed x15 -> x7, local copies, waits for them, and re-layouts: 4.6 us -> 2.06 us
    pallas_call x3 -> x2, Pallas kernels: 3.34 us -> 1.93 us  [the longest x1 1.91 us: shards(): pl.pallas_call(gather_kernel, out_shape=jax.ShapeDtypeStruct((subs, 192,...]
  transfers between devices with their start and end apart: 6 -> 6, of which waited for: 4 -> 5; matrix products, arithmetic and copies ran while one was open for 6% -> 7% of each run, Pallas kernels for 4% -> 3%
where the time goes in v5:
time: 90.6 us; the launch traced here: 89.9 us
  starting transfers between devices  46.3 us (51%)
  blocking collectives  13.8 us (15%)
  waiting for transfers between devices  13.3 us (15%)
  Pallas kernels  8.44 us (9%)
  other arithmetic  5.18 us (6%)
  local copies, waits for them, and re-layouts  2.06 us (2%)
    all_to_all x1, starting transfers between devices, shards(): spread = lax.all_to_all(totals, 'grp', 0, 0, tiled=True)  22 us
    all_to_all x1, blocking collectives, shards(): returned = lax.all_to_all(partial, 'sub', 0, 0, tiled=True)  13.8 us
    ppermute x2, starting transfers between devices, shards(): before = lax.ppermute(to_ahead, 'grp', forward)  12.3 us
    all_to_all x1, starting transfers between devices, shards(): within = lax.all_to_all(routed, 'sub', 0, 0, tiled=True)  7.66 us
    ppermute x2, waiting for transfers between devices, shards(): after = lax.ppermute(to_back, 'grp', backward)  6.71 us
    all_to_all x1, waiting for transfers between devices, shards(): within = lax.all_to_all(routed, 'sub', 0, 0, tiled=True)  5.1 us
    ppermute x2, starting transfers between devices, shards(): after = lax.ppermute(to_back, 'grp', backward)  4.34 us
    pallas_call x1, Pallas kernels, shards(): pl.pallas_call(middle_kernel, out_shape=(jax.ShapeDtypeStruct((8, atm_blo...  2.6 us
  transfers between devices with their start and end apart: 6, of which 5 were waited for; matrix products, arithmetic and copies ran while one was open for 7% of the time, Pallas kernels for 3%

profile of v5, /device:TPU:1, one launch (start us, length us, event | category | flops | bytes accessed | tf_op | source)
XLA Modules:
  0.0 89.9 jit_solution(7959471047340422691)
XLA Ops:
  0.6 1.9 %gather_slots.1 = bf16[8,192,128]{2,1,0:T(8,128)(2,1)} custom-call(s32[18,1,8]{2,1,0:T(1,128)} %bitcast.10, bf16[8,4096]{1,0:T(8,128)(2,1)} %state_hbm.1, f32[32,128]{1,0:T(8,128)} %bitcast.15), custom_call_target="tpu_custom_call" | custom-call | tf_op jit(solution)/shard_map/gather_slots/pallas_call | solution.py:232
  2.6 7.7 %all-to-all-start = ((bf16[8,192,128]{2,1,0:T(8,128)(2,1)}), bf16[8,192,128]{2,1,0:T(8,128)(2,1)S(1)}, u32[]{:S(2)}, u32[]{:S(2)}) async-start(bf16[8,192,128]{2,1,0:T(8,128)(2,1)} %gather_slots.1), calls=%async_computation | async-start | bytes 786432 | tf_op jit(solution)/shard_map/all_to_all | solution.py:250
  10.2 1.4 %copy.13 = f32[12,8]{1,0:T(8,128)} copy(f32[12,8]{0,1:T(8,128)} %param.14) | data formatting | bytes 768 | tf_op args[4]
  11.6 1.4 %convert_element_type.5 = f32[12,1024]{1,0:T(8,128)} convert(bf16[12,1024]{1,0:T(8,128)(2,1)} %param.12) | non-fusion elementwise | flops 12288 | bytes 73728 | tf_op jit(solution)/shard_map/convert_element_type | solution.py:267
  13.0 0.7 iota_compare_fusion.1
  13.7 2.2 %broadcast_select_fusion.weight = bf16[8,12,128,128]{3,2,1,0:T(8,128)(2,1)S(1)} fusion(bf16[8,12,128,128]{3,2,1,0:T(8,128)(2,1)} %param.15, pred[8,12]{1,0:T(8,128)(4,1)S(1)} %iota_compare_fusion.1), kind=kLoop, calls=%fused_computation | loop fusion | flops 1572864 | bytes 6291552 | tf_op jit(solution)/shard_map/jit(_where)/select_n | solution.py:264
  15.9 5.1 %all-to-all-done.in_ref.within_ref = bf16[8,192,128]{2,1,0:T(8,128)(2,1)S(1)} async-done(((bf16[8,192,128]{2,1,0:T(8,128)(2,1)}), bf16[8,192,128]{2,1,0:T(8,128)(2,1)S(1)}, u32[]{:S(2)}, u32[]{:S(2)}) %all-to-all-start) | async-done | bytes 393248 | tf_op jit(solution)/shard_map/all_to_all | solution.py:250
  21.0 8.8 %collective-permute-start = (bf16[8,64,128]{2,1,0:T(8,128)(2,1)S(1)}, bf16[8,64,128]{2,1,0:T(8,128)(2,1)S(1)}, u32[]{:S(2)}, u32[]{:S(2)}) collective-permute-start(bf16[8,64,128]{2,1,0:T(8,128)(2,1)S(1)} %get-tuple-element.14), channel_id=1, source_target_pairs={{0,8},{8,16},{16,24},{24,32},{32,40},{40,48},{48,56},{56,64},{64,7... | collective-permute-start | bytes 393224 | tf_op jit(solution)/shard_map/ppermute | solution.py:261
  29.8 2.4 %collective-permute-start.1 = (bf16[8,64,128]{2,1,0:T(8,128)(2,1)S(1)}, bf16[8,64,128]{2,1,0:T(8,128)(2,1)S(1)}, u32[]{:S(2)}, u32[]{:S(2)}) collective-permute-start(bf16[8,64,128]{2,1,0:T(8,128)(2,1)S(1)} %get-tuple-element.15), channel_id=1, source_target_pairs={{8,0},{16,8},{24,16},{32,24},{40,32},{48,40},{56,48},{64,56},{72,6... | collective-permute-start | bytes 393224 | tf_op jit(solution)/shard_map/ppermute | solution.py:260
  32.2 0.9 select_maximum_fusion.column_ref
  33.1 2.9 %collective-permute-done.1.after_ref = bf16[8,64,128]{2,1,0:T(8,128)(2,1)S(1)} collective-permute-done((bf16[8,64,128]{2,1,0:T(8,128)(2,1)S(1)}, bf16[8,64,128]{2,1,0:T(8,128)(2,1)S(1)}, u32[]{:S(2)}, u32[]{:S(2)}) %collective-permute-start.1) | collective-permute-done | bytes 131104 | tf_op jit(solution)/shard_map/ppermute | solution.py:260
  36.1 0.7 copy-done.2
  36.8 2.6 %remap_both_ways.1 = (bf16[8,1024]{1,0:T(8,128)(2,1)}, bf16[8,224,128]{2,1,0:T(8,128)(2,1)S(1)}) custom-call(s32[8,12]{1,0:T(8,128)S(1)} %copy-done.2, bf16[8,192,128]{2,1,0:T(8,128)(2,1)S(1)} %all-to-all-done.in_ref.within_ref, bf16[8,64,128]{2,1,0:T(8,128)(2,1)S(1)} %collective-permute-done.before_ref, ...), custom_call_target="tpu_custom_call" | custom-call | tf_op jit(solution)/shard_map/remap_both_ways/pallas_call | solution.py:274
  39.4 13.8 %all_to_all.21.in_ref = bf16[8,224,128]{2,1,0:T(8,128)(2,1)S(1)} all-to-all(bf16[8,224,128]{2,1,0:T(8,128)(2,1)S(1)} %get-tuple-element.17), channel_id=1, replica_groups=mesh['grp'=96,'sub'=8] {'sub'}, dimensions={0} | all-to-all | bytes 917504 | tf_op jit(solution)/shard_map/all_to_all | solution.py:300
  53.2 0.7 total_group.1
  53.9 22.0 %all-to-all-start.2 = ((f32[96,2,128]{2,1,0:T(2,128)}), f32[96,2,128]{2,1,0:T(2,128)S(1)}, u32[]{:S(2)}, u32[]{:S(2)}) async-start(f32[96,2,128]{2,1,0:T(2,128)} %bitcast.6), calls=%async_computation.2 | async-start | bytes 196608 | tf_op jit(solution)/shard_map/all_to_all | solution.py:318
  76.0 3.5 %collective-permute-start.2 = (bf16[8,72,128]{2,1,0:T(8,128)(2,1)S(1)}, bf16[8,72,128]{2,1,0:T(8,128)(2,1)S(1)}, u32[]{:S(2)}, u32[]{:S(2)}) collective-permute-start(bf16[8,72,128]{2,1,0:T(8,128)(2,1)S(1)} %get-tuple-element.18), channel_id=1, source_target_pairs={{0,8},{8,16},{16,24},{24,32},{32,40},{40,48},{48,56},{56,64},{64,7... | collective-permute-start | bytes 442376 | tf_op jit(solution)/shard_map/ppermute | solution.py:320
  79.5 1.9 %collective-permute-start.3 = (bf16[8,72,128]{2,1,0:T(8,128)(2,1)S(1)}, bf16[8,72,128]{2,1,0:T(8,128)(2,1)S(1)}, u32[]{:S(2)}, u32[]{:S(2)}) collective-permute-start(bf16[8,72,128]{2,1,0:T(8,128)(2,1)S(1)} %get-tuple-element.19), channel_id=1, source_target_pairs={{8,0},{16,8},{24,16},{32,24},{40,32},{48,40},{56,48},{64,56},{72,6... | collective-permute-start | bytes 442376 | tf_op jit(solution)/shard_map/ppermute | solution.py:319
  81.5 0.9 %collect_own.1 = (f32[33,8,128]{2,1,0:T(8,128)S(1)}, f32[33,8,128]{2,1,0:T(8,128)S(1)}) custom-call(s32[18,1,8]{2,1,0:T(1,128)S(1)} %bitcast.11, s32[3,1,8]{2,1,0:T(1,128)S(1)} %bitcast.13, bf16[8,72,128]{2,1,0:T(8,128)(2,1)S(1)} %get-tuple-element.20.own_ref), custom_call_target="tpu_custom_call" | custom-call | flops 1000000 | bytes 8000000 | tf_op jit(solution)/shard_map/collect_own/pallas_call | solution.py:323
  82.4 0.1 collective-permute-done.2.before_ref
  82.5 3.8 %collective-permute-done.3.after_ref = bf16[8,72,128]{2,1,0:T(8,128)(2,1)S(1)} collective-permute-done((bf16[8,72,128]{2,1,0:T(8,128)(2,1)S(1)}, bf16[8,72,128]{2,1,0:T(8,128)(2,1)S(1)}, u32[]{:S(2)}, u32[]{:S(2)}) %collective-permute-start.3) | collective-permute-done | bytes 147488 | tf_op jit(solution)/shard_map/ppermute | solution.py:319
  86.3 1.7 %collect_flux.1 = (bf16[12,4096]{1,0:T(8,128)(2,1)}, s32[8,128]{1,0:T(8,128)S(1)}) custom-call(s32[18,1,8]{2,1,0:T(1,128)S(1)} %bitcast.12, s32[3,1,8]{2,1,0:T(1,128)S(1)} %bitcast.14, bf16[8,72,128]{2,1,0:T(8,128)(2,1)S(1)} %collective-permute-done.2.before_ref, bf16[8,72,128]{2,1,0:T(8,128)(2,1)S(1)} %collective-permute-done.3.after_ref, ...), custom_call_target="tpu_custom_call" | custom-call | flops 1000000 | bytes 8000000 | tf_op jit(solution)/shard_map/collect_flux/pallas_call | solution.py:332
  88.0 1.4 %all-to-all-done.2 = f32[96,2,128]{2,1,0:T(2,128)S(1)} async-done(((f32[96,2,128]{2,1,0:T(2,128)}), f32[96,2,128]{2,1,0:T(2,128)S(1)}, u32[]{:S(2)}, u32[]{:S(2)}) %all-to-all-start.2) | async-done | bytes 98336 | tf_op jit(solution)/shard_map/all_to_all | solution.py:318
  89.4 0.5 total_all.1
  (9 shorter events, 0.1 us)
Async XLA Ops:
  2.6 18.4 %all-to-all-start = ((bf16[8,192,128]{2,1,0:T(8,128)(2,1)}), bf16[8,192,128]{2,1,0:T(8,128)(2,1)S(1)}, u32[]{:S(2)}, u32[]{:S(2)}) async-start(bf16[8,192,128]{2,1,0:T(8,128)(2,1)} %gather_slots.1), calls=%async_computation | async-start | bytes 786432 | tf_op jit(solution)/shard_map/all_to_all | solution.py:250
  21.0 60.5 %copy-start = (s32[1,3,8,6]{2,0,3,1:T(1,128)S(1)}, s32[1,3,8,6]{2,0,3,1:T(1,128)}, u32[]{:S(2)}) copy-start(s32[1,3,8,6]{2,0,3,1:T(1,128)} %param.16) | copy-start | bytes 1732
  21.0 60.5 %copy-start.1 = (s32[1,3,8]{2,0,1:T(1,128)S(1)}, s32[1,3,8]{2,0,1:T(1,128)}, u32[]{:S(2)}) copy-start(s32[1,3,8]{2,0,1:T(1,128)} %param.17) | copy-start | bytes 292
  21.0 12.1 %collective-permute-start = (bf16[8,64,128]{2,1,0:T(8,128)(2,1)S(1)}, bf16[8,64,128]{2,1,0:T(8,128)(2,1)S(1)}, u32[]{:S(2)}, u32[]{:S(2)}) collective-permute-start(bf16[8,64,128]{2,1,0:T(8,128)(2,1)S(1)} %get-tuple-element.14), channel_id=1, source_target_pairs={{0,8},{8,16},{16,24},{24,32},{32,40},{40,48},{48,56},{56,64},{64,7... | collective-permute-start | bytes 393224 | tf_op jit(solution)/shard_map/ppermute | solution.py:261
  29.8 6.3 %collective-permute-start.1 = (bf16[8,64,128]{2,1,0:T(8,128)(2,1)S(1)}, bf16[8,64,128]{2,1,0:T(8,128)(2,1)S(1)}, u32[]{:S(2)}, u32[]{:S(2)}) collective-permute-start(bf16[8,64,128]{2,1,0:T(8,128)(2,1)S(1)} %get-tuple-element.15), channel_id=1, source_target_pairs={{8,0},{16,8},{24,16},{32,24},{40,32},{48,40},{56,48},{64,56},{72,6... | collective-permute-start | bytes 393224 | tf_op jit(solution)/shard_map/ppermute | solution.py:260
  36.1 0.7 copy-start.2
  53.9 35.5 %all-to-all-start.2 = ((f32[96,2,128]{2,1,0:T(2,128)}), f32[96,2,128]{2,1,0:T(2,128)S(1)}, u32[]{:S(2)}, u32[]{:S(2)}) async-start(f32[96,2,128]{2,1,0:T(2,128)} %bitcast.6), calls=%async_computation.2 | async-start | bytes 196608 | tf_op jit(solution)/shard_map/all_to_all | solution.py:318
  76.0 6.5 %collective-permute-start.2 = (bf16[8,72,128]{2,1,0:T(8,128)(2,1)S(1)}, bf16[8,72,128]{2,1,0:T(8,128)(2,1)S(1)}, u32[]{:S(2)}, u32[]{:S(2)}) collective-permute-start(bf16[8,72,128]{2,1,0:T(8,128)(2,1)S(1)} %get-tuple-element.18), channel_id=1, source_target_pairs={{0,8},{8,16},{16,24},{24,32},{32,40},{40,48},{48,56},{56,64},{64,7... | collective-permute-start | bytes 442376 | tf_op jit(solution)/shard_map/ppermute | solution.py:320
  79.5 6.8 %collective-permute-start.3 = (bf16[8,72,128]{2,1,0:T(8,128)(2,1)S(1)}, bf16[8,72,128]{2,1,0:T(8,128)(2,1)S(1)}, u32[]{:S(2)}, u32[]{:S(2)}) collective-permute-start(bf16[8,72,128]{2,1,0:T(8,128)(2,1)S(1)} %get-tuple-element.19), channel_id=1, source_target_pairs={{8,0},{16,8},{24,16},{32,24},{40,32},{48,40},{56,48},{64,56},{72,6... | collective-permute-start | bytes 442376 | tf_op jit(solution)/shard_map/ppermute | solution.py:319

commit v6 on v5

--- a/solution.py
+++ b/solution.py
@@ -50,16 +50,17 @@
             out_ref[k, o * 64 + 48 : o * 64 + 64, :] = rows[o * subs + k].astype(BF16)
 
 
-def forward_kernel(in_ref, back_out, ahead_out):
-    back_out[...] = in_ref[:, 0:64, :]
-    ahead_out[...] = in_ref[:, 128:192, :]
+def forward_kernel(in_ref, chip_out, core_out):
+    start = pl.multiple_of(lax.axis_index("grp") % 2 * 128, 128)
+    chip_out[...] = in_ref[:, pl.ds(start, 64), :]
+    core_out[...] = in_ref[:, pl.ds(128 - start, 64), :]
 
 
 def middle_kernel(
     slot_ref,
     within_ref,
-    before_ref,
-    after_ref,
+    chip_ref,
+    core_ref,
     column_ref,
     weight,
     state_out,
@@ -72,12 +73,13 @@
 ):
     blocks, links = weight.shape[0], weight.shape[1]
     subs = within_ref.shape[0]
+    far = lax.axis_index("grp") % 2 * 2
     acc_low[...] = jnp.zeros_like(acc_low)
     acc_high[...] = jnp.zeros_like(acc_high)
     for j in range(subs):
-        for p, part in enumerate((before_ref[j], within_ref[j, 64:128, :], after_ref[j])):
+        for p, part in ((far, chip_ref[j]), (1, within_ref[j, 64:128, :]), (2 - far, core_ref[j])):
             tiles = part.astype(F32).reshape(8, 8, 128)
-            arrived[(p * subs + j) * 8 : (p * subs + j + 1) * 8] = tiles
+            arrived[pl.ds((p * subs + j) * 8, 8)] = tiles
     for a in range(blocks):
         for link in range(links):
             slot = slot_ref[a, link]
@@ -155,11 +157,14 @@
         part_out[j] = out.astype(BF16)
 
 
-def split_kernel(in_ref, back_out, own_out, ahead_out):
+def split_kernel(in_ref, chip_out, own_out, core_out):
+    odd = lax.axis_index("grp") % 2 == 1
     for k in range(in_ref.shape[0]):
         part = in_ref[k].astype(F32)
-        for p, ref in enumerate((back_out, own_out, ahead_out)):
-            ref[k] = part[p * 72 : p * 72 + 72].astype(BF16)
+        back, own, ahead = (part[p * 72 : p * 72 + 72] for p in range(3))
+        chip_out[k] = jnp.where(odd, ahead, back).astype(BF16)
+        own_out[k] = own.astype(BF16)
+        core_out[k] = jnp.where(odd, back, ahead).astype(BF16)
 
 
 def group_total_kernel(in_ref, total_out):
@@ -189,12 +194,13 @@
     add_slots((1,), (own_ref,), block, count, (low,), (high,))
 
 
-def final_kernel(block, count, before_ref, after_ref, own_low, own_high, flux_out, done_out, low, high, more_low, more_high):
+def final_kernel(block, count, chip_ref, core_ref, own_low, own_high, flux_out, done_out, low, high, more_low, more_high):
     blocks = flux_out.shape[1] // 128
     for ref in (low, high, more_low, more_high):
         ref[...] = jnp.zeros_like(ref)
+    far = lax.axis_index("grp") % 2 * 2
     add_slots(
-        (0, 2), (before_ref, after_ref), block, count, (low, more_low), (high, more_high)
+        (far, 2 - far), (chip_ref, core_ref), block, count, (low, more_low), (high, more_high)
     )
     for b in range(blocks):
         upper = high[b] + more_high[b] + own_high[b]
@@ -224,8 +230,8 @@
     atm_blocks, links, width = remap_weight.shape[:3]
     ocean_blocks = ocean_state.shape[1] // width
     groups, subs = lax.axis_size("grp"), lax.axis_size("sub")
-    forward = [(i, (i + 1) % groups) for i in range(groups)]
-    backward = [(target, source) for source, target in forward]
+    across_chips = [(i, (i + 1 if i % 2 else i - 1) % groups) for i in range(groups)]
+    across_cores = [(i, i ^ 1) for i in range(groups)]
     chosen = send_block.transpose(1, 3, 0, 2).reshape(18, 1, subs)
     counts = send_count.transpose(1, 0, 2)
 
@@ -249,7 +255,7 @@
     )(chosen, ocean_state, ocean_area.reshape(ocean_blocks, width))
     within = lax.all_to_all(routed, "sub", 0, 0, tiled=True)
     route = jax.ShapeDtypeStruct((subs, 64, width), BF16)
-    to_back, to_ahead = pl.pallas_call(
+    to_chip, to_core = pl.pallas_call(
         forward_kernel,
         out_shape=(route, route),
         in_specs=[VMEM],
@@ -257,8 +263,8 @@
         compiler_params=PART,
         name="forward_routes",
     )(within)
-    after = lax.ppermute(to_back, "grp", backward)
-    before = lax.ppermute(to_ahead, "grp", forward)
+    from_chip = lax.ppermute(to_chip, "grp", across_chips)
+    from_core = lax.ppermute(to_core, "grp", across_cores)
 
     live = lax.broadcasted_iota(jnp.int32, link_slot.shape, 1) < link_count[:, None]
     weight = jnp.where(live[:, :, None, None], remap_weight, jnp.zeros((), BF16))
@@ -291,8 +297,8 @@
     )(
         link_slot,
         within,
-        before,
-        after,
+        from_chip,
+        from_core,
         columns,
         weight,
     )
@@ -307,7 +313,7 @@
         compiler_params=PART,
         name="total_group",
     )(returned)
-    to_back, own_flux, to_ahead = pl.pallas_call(
+    to_chip, own_flux, to_core = pl.pallas_call(
         split_kernel,
         out_shape=(route, route, route),
         in_specs=[VMEM],
@@ -316,8 +322,8 @@
         name="split_routes",
     )(returned)
     spread = lax.all_to_all(totals, "grp", 0, 0, tiled=True)
-    after = lax.ppermute(to_back, "grp", backward)
-    before = lax.ppermute(to_ahead, "grp", forward)
+    from_chip = lax.ppermute(to_chip, "grp", across_chips)
+    from_core = lax.ppermute(to_core, "grp", across_cores)
 
     sums = jax.ShapeDtypeStruct((ocean_blocks + 1, 8, width), F32)
     own_low, own_high = pl.pallas_call(
@@ -346,7 +352,7 @@
         compiler_params=PART,
         cost_estimate=pl.CostEstimate(flops=10**6, bytes_accessed=8 * 10**6, transcendentals=0),
         name="collect_flux",
-    )(chosen, counts, before, after, own_low, own_high)
+    )(chosen, counts, from_chip, from_core, own_low, own_high)
     scale = 1.0 / math.sqrt(groups * subs * atm_blocks * width)
     imbalance = pl.pallas_call(
         functools.partial(total_kernel, scale),

time: 90.6 us -> 88.8 us (0.980)
  waiting for transfers between devices: 13.3 us -> 6.4 us
  blocking collectives: 13.8 us -> 18.9 us
    all_to_all x1, starting transfers between devices: 22 us -> 6.91 us  [shards(): spread = lax.all_to_all(totals, 'grp', 0, 0, tiled=True)]
    ppermute x4, starting transfers between devices: 16.6 us -> 31.7 us  [the longest x2 19.4 us: shards(): from_core = lax.ppermute(to_core, 'grp', across_cores)]
    ppermute x4, waiting for transfers between devices: 6.81 us -> 0.08 us  [the longest x2 0.08 us: shards(): from_core = lax.ppermute(to_core, 'grp', across_cores)]
    all_to_all x1, blocking collectives: 13.8 us -> 18.9 us  [shards(): returned = lax.all_to_all(partial, 'sub', 0, 0, tiled=True)]
  transfers between devices with their start and end apart: 6 -> 6, of which waited for: 5 -> 2; matrix products, arithmetic and copies ran while one was open for 7% -> 7% of each run, Pallas kernels for 3% -> 3%
where the time goes in v6:
time: 88.8 us; the launch traced here: 88.1 us
  starting transfers between devices  46.2 us (52%)
  blocking collectives  18.9 us (21%)
  Pallas kernels  8.49 us (10%)
  waiting for transfers between devices  6.4 us (7%)
  other arithmetic  5.18 us (6%)
  local copies, waits for them, and re-layouts  2.06 us (2%)
    ppermute x2, starting transfers between devices, shards(): from_core = lax.ppermute(to_core, 'grp', across_cores)  19.4 us
    all_to_all x1, blocking collectives, shards(): returned = lax.all_to_all(partial, 'sub', 0, 0, tiled=True)  18.9 us
    ppermute x2, starting transfers between devices, shards(): from_chip = lax.ppermute(to_chip, 'grp', across_chips)  12.3 us
    all_to_all x1, starting transfers between devices, shards(): within = lax.all_to_all(routed, 'sub', 0, 0, tiled=True)  7.66 us
    all_to_all x1, starting transfers between devices, shards(): spread = lax.all_to_all(totals, 'grp', 0, 0, tiled=True)  6.91 us
    all_to_all x1, waiting for transfers between devices, shards(): within = lax.all_to_all(routed, 'sub', 0, 0, tiled=True)  5.1 us
    pallas_call x1, Pallas kernels, shards(): pl.pallas_call(middle_kernel, out_shape=(jax.ShapeDtypeStruct((8, atm_blo...  2.64 us
    select_n x1, other arithmetic, shards(): jnp.where(live[:, :, None, None], remap_weight, jnp.zeros((), BF16))  2.17 us
  transfers between devices with their start and end apart: 6, of which 2 were waited for; matrix products, arithmetic and copies ran while one was open for 7% of the time, Pallas kernels for 3%

profile of v6, /device:TPU:1, one launch (start us, length us, event | category | flops | bytes accessed | tf_op | source)
XLA Modules:
  0.0 88.1 jit_solution(2103000739157432918)
XLA Ops:
  0.6 1.9 %gather_slots.1 = bf16[8,192,128]{2,1,0:T(8,128)(2,1)} custom-call(s32[18,1,8]{2,1,0:T(1,128)} %bitcast.10, bf16[8,4096]{1,0:T(8,128)(2,1)} %state_hbm.1, f32[32,128]{1,0:T(8,128)} %bitcast.15), custom_call_target="tpu_custom_call" | custom-call | tf_op jit(solution)/shard_map/gather_slots/pallas_call | solution.py:238
  2.6 7.7 %all-to-all-start = ((bf16[8,192,128]{2,1,0:T(8,128)(2,1)}), bf16[8,192,128]{2,1,0:T(8,128)(2,1)S(1)}, u32[]{:S(2)}, u32[]{:S(2)}) async-start(bf16[8,192,128]{2,1,0:T(8,128)(2,1)} %gather_slots.1), calls=%async_computation | async-start | bytes 786432 | tf_op jit(solution)/shard_map/all_to_all | solution.py:256
  10.2 1.4 %copy.13 = f32[12,8]{1,0:T(8,128)} copy(f32[12,8]{0,1:T(8,128)} %param.14) | data formatting | bytes 768 | tf_op args[4]
  11.6 1.4 %convert_element_type.5 = f32[12,1024]{1,0:T(8,128)} convert(bf16[12,1024]{1,0:T(8,128)(2,1)} %param.12) | non-fusion elementwise | flops 12288 | bytes 73728 | tf_op jit(solution)/shard_map/convert_element_type | solution.py:273
  13.0 0.7 iota_compare_fusion.1
  13.7 2.2 %broadcast_select_fusion.weight = bf16[8,12,128,128]{3,2,1,0:T(8,128)(2,1)S(1)} fusion(bf16[8,12,128,128]{3,2,1,0:T(8,128)(2,1)} %param.15, pred[8,12]{1,0:T(8,128)(4,1)S(1)} %iota_compare_fusion.1), kind=kLoop, calls=%fused_computation | loop fusion | flops 1572864 | bytes 6291552 | tf_op jit(solution)/shard_map/jit(_where)/select_n | solution.py:270
  15.9 5.1 %all-to-all-done.in_ref.within_ref = bf16[8,192,128]{2,1,0:T(8,128)(2,1)S(1)} async-done(((bf16[8,192,128]{2,1,0:T(8,128)(2,1)}), bf16[8,192,128]{2,1,0:T(8,128)(2,1)S(1)}, u32[]{:S(2)}, u32[]{:S(2)}) %all-to-all-start) | async-done | bytes 393248 | tf_op jit(solution)/shard_map/all_to_all | solution.py:256
  21.0 8.8 %collective-permute-start = (bf16[8,64,128]{2,1,0:T(8,128)(2,1)S(1)}, bf16[8,64,128]{2,1,0:T(8,128)(2,1)S(1)}, u32[]{:S(2)}, u32[]{:S(2)}) collective-permute-start(bf16[8,64,128]{2,1,0:T(8,128)(2,1)S(1)} %get-tuple-element.14), channel_id=1, source_target_pairs={{0,760},{8,16},{16,8},{24,32},{32,24},{40,48},{48,40},{56,64},{64,... | collective-permute-start | bytes 393224 | tf_op jit(solution)/shard_map/ppermute | solution.py:266
  29.8 13.5 %collective-permute-start.1 = (bf16[8,64,128]{2,1,0:T(8,128)(2,1)S(1)}, bf16[8,64,128]{2,1,0:T(8,128)(2,1)S(1)}, u32[]{:S(2)}, u32[]{:S(2)}) collective-permute-start(bf16[8,64,128]{2,1,0:T(8,128)(2,1)S(1)} %get-tuple-element.15), channel_id=1, source_target_pairs={{0,8},{8,0},{16,24},{24,16},{32,40},{40,32},{48,56},{56,48},{64,72... | collective-permute-start | bytes 393224 | tf_op jit(solution)/shard_map/ppermute | solution.py:267
  43.3 0.9 %select_maximum_fusion.column_ref = f32[16,1152]{1,0:T(8,128)S(1)} fusion(f32[12,8]{1,0:T(8,128)} %copy.13, f32[3,1024]{1,0:T(4,128)S(1)} %broadcast_in_dim.21, f32[1,1024]{1,0:T(1,128)} %bitcast.16, f32[12,1024]{1,0:T(8,128)} %convert_element_type.5), kind=kLoop, calls=%fused_computation.1 | loop fusion | flops 92160 | bytes 139648 | tf_op jit(solution)/shard_map/concatenate | solution.py:271
  44.2 0.0 collective-permute-done.1.core_ref
  44.2 0.7 copy-done.2
  44.9 2.6 %remap_both_ways.1 = (bf16[8,1024]{1,0:T(8,128)(2,1)}, bf16[8,224,128]{2,1,0:T(8,128)(2,1)S(1)}) custom-call(s32[8,12]{1,0:T(8,128)S(1)} %copy-done.2, bf16[8,192,128]{2,1,0:T(8,128)(2,1)S(1)} %all-to-all-done.in_ref.within_ref, bf16[8,64,128]{2,1,0:T(8,128)(2,1)S(1)} %collective-permute-done.chip_ref, ...), custom_call_target="tpu_custom_call" | custom-call | tf_op jit(solution)/shard_map/remap_both_ways/pallas_call | solution.py:280
  47.6 18.9 %all_to_all.21.in_ref = bf16[8,224,128]{2,1,0:T(8,128)(2,1)S(1)} all-to-all(bf16[8,224,128]{2,1,0:T(8,128)(2,1)S(1)} %get-tuple-element.17), channel_id=1, replica_groups=mesh['grp'=96,'sub'=8] {'sub'}, dimensions={0} | all-to-all | bytes 917504 | tf_op jit(solution)/shard_map/all_to_all | solution.py:306
  66.5 0.7 total_group.1
  67.2 6.9 %all-to-all-start.2 = ((f32[96,2,128]{2,1,0:T(2,128)}), f32[96,2,128]{2,1,0:T(2,128)S(1)}, u32[]{:S(2)}, u32[]{:S(2)}) async-start(f32[96,2,128]{2,1,0:T(2,128)} %bitcast.6), calls=%async_computation.2 | async-start | bytes 196608 | tf_op jit(solution)/shard_map/all_to_all | solution.py:324
  74.1 0.1 split_routes.1
  74.2 3.5 %collective-permute-start.2 = (bf16[8,72,128]{2,1,0:T(8,128)(2,1)S(1)}, bf16[8,72,128]{2,1,0:T(8,128)(2,1)S(1)}, u32[]{:S(2)}, u32[]{:S(2)}) collective-permute-start(bf16[8,72,128]{2,1,0:T(8,128)(2,1)S(1)} %get-tuple-element.18), channel_id=1, source_target_pairs={{0,760},{8,16},{16,8},{24,32},{32,24},{40,48},{48,40},{56,64},{64,... | collective-permute-start | bytes 442376 | tf_op jit(solution)/shard_map/ppermute | solution.py:325
  77.7 5.9 %collective-permute-start.3 = (bf16[8,72,128]{2,1,0:T(8,128)(2,1)S(1)}, bf16[8,72,128]{2,1,0:T(8,128)(2,1)S(1)}, u32[]{:S(2)}, u32[]{:S(2)}) collective-permute-start(bf16[8,72,128]{2,1,0:T(8,128)(2,1)S(1)} %get-tuple-element.19), channel_id=1, source_target_pairs={{0,8},{8,0},{16,24},{24,16},{32,40},{40,32},{48,56},{56,48},{64,72... | collective-permute-start | bytes 442376 | tf_op jit(solution)/shard_map/ppermute | solution.py:326
  83.7 0.9 %collect_own.1 = (f32[33,8,128]{2,1,0:T(8,128)S(1)}, f32[33,8,128]{2,1,0:T(8,128)S(1)}) custom-call(s32[18,1,8]{2,1,0:T(1,128)S(1)} %bitcast.11, s32[3,1,8]{2,1,0:T(1,128)S(1)} %bitcast.13, bf16[8,72,128]{2,1,0:T(8,128)(2,1)S(1)} %get-tuple-element.20.own_ref), custom_call_target="tpu_custom_call" | custom-call | flops 1000000 | bytes 8000000 | tf_op jit(solution)/shard_map/collect_own/pallas_call | solution.py:329
  84.6 0.0 collective-permute-done.3.core_ref
  84.6 1.7 %collect_flux.1 = (bf16[12,4096]{1,0:T(8,128)(2,1)}, s32[8,128]{1,0:T(8,128)S(1)}) custom-call(s32[18,1,8]{2,1,0:T(1,128)S(1)} %bitcast.12, s32[3,1,8]{2,1,0:T(1,128)S(1)} %bitcast.14, bf16[8,72,128]{2,1,0:T(8,128)(2,1)S(1)} %collective-permute-done.2.chip_ref, bf16[8,72,128]{2,1,0:T(8,128)(2,1)S(1)} %collective-permute-done.3.core_ref, ...), custom_call_target="tpu_custom_call" | custom-call | flops 1000000 | bytes 8000000 | tf_op jit(solution)/shard_map/collect_flux/pallas_call | solution.py:338
  86.3 1.2 %all-to-all-done.2 = f32[96,2,128]{2,1,0:T(2,128)S(1)} async-done(((f32[96,2,128]{2,1,0:T(2,128)}), f32[96,2,128]{2,1,0:T(2,128)S(1)}, u32[]{:S(2)}, u32[]{:S(2)}) %all-to-all-start.2) | async-done | bytes 98336 | tf_op jit(solution)/shard_map/all_to_all | solution.py:324
  87.5 0.5 total_all.1
  (9 shorter events, 0.0 us)
Async XLA Ops:
  2.6 18.4 %all-to-all-start = ((bf16[8,192,128]{2,1,0:T(8,128)(2,1)}), bf16[8,192,128]{2,1,0:T(8,128)(2,1)S(1)}, u32[]{:S(2)}, u32[]{:S(2)}) async-start(bf16[8,192,128]{2,1,0:T(8,128)(2,1)} %gather_slots.1), calls=%async_computation | async-start | bytes 786432 | tf_op jit(solution)/shard_map/all_to_all | solution.py:256
  21.0 62.6 %copy-start = (s32[1,3,8,6]{2,0,3,1:T(1,128)S(1)}, s32[1,3,8,6]{2,0,3,1:T(1,128)}, u32[]{:S(2)}) copy-start(s32[1,3,8,6]{2,0,3,1:T(1,128)} %param.16) | copy-start | bytes 1732
  21.0 62.6 %copy-start.1 = (s32[1,3,8]{2,0,1:T(1,128)S(1)}, s32[1,3,8]{2,0,1:T(1,128)}, u32[]{:S(2)}) copy-start(s32[1,3,8]{2,0,1:T(1,128)} %param.17) | copy-start | bytes 292
  21.0 23.2 %collective-permute-start = (bf16[8,64,128]{2,1,0:T(8,128)(2,1)S(1)}, bf16[8,64,128]{2,1,0:T(8,128)(2,1)S(1)}, u32[]{:S(2)}, u32[]{:S(2)}) collective-permute-start(bf16[8,64,128]{2,1,0:T(8,128)(2,1)S(1)} %get-tuple-element.14), channel_id=1, source_target_pairs={{0,760},{8,16},{16,8},{24,32},{32,24},{40,48},{48,40},{56,64},{64,... | collective-permute-start | bytes 393224 | tf_op jit(solution)/shard_map/ppermute | solution.py:266
  29.8 14.4 %collective-permute-start.1 = (bf16[8,64,128]{2,1,0:T(8,128)(2,1)S(1)}, bf16[8,64,128]{2,1,0:T(8,128)(2,1)S(1)}, u32[]{:S(2)}, u32[]{:S(2)}) collective-permute-start(bf16[8,64,128]{2,1,0:T(8,128)(2,1)S(1)} %get-tuple-element.15), channel_id=1, source_target_pairs={{0,8},{8,0},{16,24},{24,16},{32,40},{40,32},{48,56},{56,48},{64,72... | collective-permute-start | bytes 393224 | tf_op jit(solution)/shard_map/ppermute | solution.py:267
  44.2 0.7 copy-start.2
  67.2 20.4 %all-to-all-start.2 = ((f32[96,2,128]{2,1,0:T(2,128)}), f32[96,2,128]{2,1,0:T(2,128)S(1)}, u32[]{:S(2)}, u32[]{:S(2)}) async-start(f32[96,2,128]{2,1,0:T(2,128)} %bitcast.6), calls=%async_computation.2 | async-start | bytes 196608 | tf_op jit(solution)/shard_map/all_to_all | solution.py:324
  74.2 10.4 %collective-permute-start.2 = (bf16[8,72,128]{2,1,0:T(8,128)(2,1)S(1)}, bf16[8,72,128]{2,1,0:T(8,128)(2,1)S(1)}, u32[]{:S(2)}, u32[]{:S(2)}) collective-permute-start(bf16[8,72,128]{2,1,0:T(8,128)(2,1)S(1)} %get-tuple-element.18), channel_id=1, source_target_pairs={{0,760},{8,16},{16,8},{24,32},{32,24},{40,48},{48,40},{56,64},{64,... | collective-permute-start | bytes 442376 | tf_op jit(solution)/shard_map/ppermute | solution.py:325
  77.7 6.9 %collective-permute-start.3 = (bf16[8,72,128]{2,1,0:T(8,128)(2,1)S(1)}, bf16[8,72,128]{2,1,0:T(8,128)(2,1)S(1)}, u32[]{:S(2)}, u32[]{:S(2)}) collective-permute-start(bf16[8,72,128]{2,1,0:T(8,128)(2,1)S(1)} %get-tuple-element.19), channel_id=1, source_target_pairs={{0,8},{8,0},{16,24},{24,16},{32,40},{40,32},{48,56},{56,48},{64,72... | collective-permute-start | bytes 442376 | tf_op jit(solution)/shard_map/ppermute | solution.py:326

commit v7 on v6

--- a/solution.py
+++ b/solution.py
@@ -263,18 +263,20 @@
         compiler_params=PART,
         name="forward_routes",
     )(within)
-    from_chip = lax.ppermute(to_chip, "grp", across_chips)
-    from_core = lax.ppermute(to_core, "grp", across_cores)
 
     live = lax.broadcasted_iota(jnp.int32, link_slot.shape, 1) < link_count[:, None]
     weight = jnp.where(live[:, :, None, None], remap_weight, jnp.zeros((), BF16))
+    flux_wide, to_chip, to_core = lax.optimization_barrier((atm_flux.astype(F32), to_chip, to_core))
     columns = jnp.concatenate(
         [
-            jnp.concatenate([atm_flux.astype(F32), atm_area[None], jnp.zeros((3, atm_area.shape[0]), F32)], axis=0),
+            jnp.concatenate([flux_wide, atm_area[None], jnp.zeros((3, atm_area.shape[0]), F32)], axis=0),
             jnp.pad(coupling, ((0, 4), (0, width - coupling.shape[1]))),
         ],
         axis=1,
     )
+
+    from_chip = lax.ppermute(to_chip, "grp", across_chips)
+    from_core = lax.ppermute(to_core, "grp", across_cores)
 
     slots = 18 * subs
     state_on_atm, partial = pl.pallas_call(
@@ -295,7 +297,7 @@
         compiler_params=PART,
         name="remap_both_ways",
     )(
-        link_slot,
+        jnp.where(live, link_slot, 0),
         within,
         from_chip,
         from_core,

time: 88.8 us -> 88.2 us (level)
  waiting for transfers between devices: 6.4 us -> 4.94 us
    unnamed x7 -> x5, local copies, waits for them, and re-layouts: 2.06 us -> 2.04 us
  transfers between devices with their start and end apart: 6 -> 6, of which waited for: 2 -> 2; matrix products, arithmetic and copies ran while one was open for 7% -> 8% of each run, Pallas kernels for 3% -> 3%
where the time goes in v7:
time: 88.2 us; the launch traced here: 87.4 us
  starting transfers between devices  46.3 us (52%)
  blocking collectives  18.9 us (21%)
  Pallas kernels  8.55 us (10%)
  other arithmetic  5.94 us (7%)
  waiting for transfers between devices  4.94 us (6%)
  local copies, waits for them, and re-layouts  2.05 us (2%)
    ppermute x2, starting transfers between devices, shards(): from_core = lax.ppermute(to_core, 'grp', across_cores)  19.4 us
    all_to_all x1, blocking collectives, shards(): returned = lax.all_to_all(partial, 'sub', 0, 0, tiled=True)  18.9 us
    ppermute x2, starting transfers between devices, shards(): from_chip = lax.ppermute(to_chip, 'grp', across_chips)  12.3 us
    all_to_all x1, starting transfers between devices, shards(): within = lax.all_to_all(routed, 'sub', 0, 0, tiled=True)  7.66 us
    all_to_all x1, starting transfers between devices, shards(): spread = lax.all_to_all(totals, 'grp', 0, 0, tiled=True)  6.91 us
    all_to_all x1, waiting for transfers between devices, shards(): within = lax.all_to_all(routed, 'sub', 0, 0, tiled=True)  4.34 us
    pallas_call x1, Pallas kernels, shards(): pl.pallas_call(middle_kernel, out_shape=(jax.ShapeDtypeStruct((8, atm_blo...  2.69 us
    select_n x1, other arithmetic, shards(): jnp.where(live[:, :, None, None], remap_weight, jnp.zeros((), BF16))  2.17 us
  transfers between devices with their start and end apart: 6, of which 2 were waited for; matrix products, arithmetic and copies ran while one was open for 8% of the time, Pallas kernels for 3%

profile of v7, /device:TPU:1, one launch (start us, length us, event | category | flops | bytes accessed | tf_op | source)
XLA Modules:
  0.0 87.4 jit_solution(18190872434321486653)
XLA Ops:
  0.6 1.9 %gather_slots.1 = bf16[8,192,128]{2,1,0:T(8,128)(2,1)} custom-call(s32[18,1,8]{2,1,0:T(1,128)} %bitcast.10, bf16[8,4096]{1,0:T(8,128)(2,1)} %state_hbm.1, f32[32,128]{1,0:T(8,128)} %bitcast.15), custom_call_target="tpu_custom_call" | custom-call | tf_op jit(solution)/shard_map/gather_slots/pallas_call | solution.py:238
  2.5 7.7 %all-to-all-start = ((bf16[8,192,128]{2,1,0:T(8,128)(2,1)}), bf16[8,192,128]{2,1,0:T(8,128)(2,1)S(1)}, u32[]{:S(2)}, u32[]{:S(2)}) async-start(bf16[8,192,128]{2,1,0:T(8,128)(2,1)} %gather_slots.1), calls=%async_computation | async-start | bytes 786432 | tf_op jit(solution)/shard_map/all_to_all | solution.py:256
  10.2 0.7 iota_compare_fusion.1
  10.9 1.4 %copy.13 = f32[12,8]{1,0:T(8,128)} copy(f32[12,8]{0,1:T(8,128)} %param.14) | data formatting | bytes 768 | tf_op args[4]
  12.3 1.4 %convert_element_type.5 = f32[12,1024]{1,0:T(8,128)} convert(bf16[12,1024]{1,0:T(8,128)(2,1)} %param.12) | non-fusion elementwise | flops 12288 | bytes 73728 | tf_op jit(solution)/shard_map/convert_element_type | solution.py:269
  13.7 0.8 broadcast_select_fusion.1.slot_ref
  14.4 2.2 %broadcast_select_fusion.weight = bf16[8,12,128,128]{3,2,1,0:T(8,128)(2,1)S(1)} fusion(bf16[8,12,128,128]{3,2,1,0:T(8,128)(2,1)} %param.15, pred[8,12]{1,0:T(8,128)(4,1)S(1)} %iota_compare_fusion.1), kind=kLoop, calls=%fused_computation | loop fusion | flops 1572864 | bytes 6291552 | tf_op jit(solution)/shard_map/jit(_where)/select_n | solution.py:268
  16.6 4.3 %all-to-all-done.in_ref.within_ref = bf16[8,192,128]{2,1,0:T(8,128)(2,1)S(1)} async-done(((bf16[8,192,128]{2,1,0:T(8,128)(2,1)}), bf16[8,192,128]{2,1,0:T(8,128)(2,1)S(1)}, u32[]{:S(2)}, u32[]{:S(2)}) %all-to-all-start) | async-done | bytes 393248 | tf_op jit(solution)/shard_map/all_to_all | solution.py:256
  21.0 8.8 %collective-permute-start = (bf16[8,64,128]{2,1,0:T(8,128)(2,1)S(1)}, bf16[8,64,128]{2,1,0:T(8,128)(2,1)S(1)}, u32[]{:S(2)}, u32[]{:S(2)}) collective-permute-start(bf16[8,64,128]{2,1,0:T(8,128)(2,1)S(1)} %get-tuple-element.19), channel_id=1, source_target_pairs={{0,760},{8,16},{16,8},{24,32},{32,24},{40,48},{48,40},{56,64},{64,... | collective-permute-start | bytes 393224 | tf_op jit(solution)/shard_map/ppermute | solution.py:278
  29.8 13.5 %collective-permute-start.1 = (bf16[8,64,128]{2,1,0:T(8,128)(2,1)S(1)}, bf16[8,64,128]{2,1,0:T(8,128)(2,1)S(1)}, u32[]{:S(2)}, u32[]{:S(2)}) collective-permute-start(bf16[8,64,128]{2,1,0:T(8,128)(2,1)S(1)} %get-tuple-element.20), channel_id=1, source_target_pairs={{0,8},{8,0},{16,24},{24,16},{32,40},{40,32},{48,56},{56,48},{64,72... | collective-permute-start | bytes 393224 | tf_op jit(solution)/shard_map/ppermute | solution.py:279
  43.3 0.9 %select_maximum_fusion.column_ref = f32[16,1152]{1,0:T(8,128)S(1)} fusion(f32[12,8]{1,0:T(8,128)} %copy.13, f32[3,1024]{1,0:T(4,128)S(1)} %broadcast_in_dim.26, f32[1,1024]{1,0:T(1,128)} %bitcast.16, f32[12,1024]{1,0:T(8,128)} %convert_element_type.5), kind=kLoop, calls=%fused_computation.1 | loop fusion | flops 92160 | bytes 139648 | tf_op jit(solution)/shard_map/concatenate | solution.py:270
  44.2 0.0 collective-permute-done.1.core_ref
  44.2 2.7 %remap_both_ways.1 = (bf16[8,1024]{1,0:T(8,128)(2,1)}, bf16[8,224,128]{2,1,0:T(8,128)(2,1)S(1)}) custom-call(s32[8,12]{1,0:T(8,128)S(1)} %broadcast_select_fusion.1.slot_ref, bf16[8,192,128]{2,1,0:T(8,128)(2,1)S(1)} %all-to-all-done.in_ref.within_ref, bf16[8,64,128]{2,1,0:T(8,128)(2,1)S(1)} %collective-permute-done.chip_ref, ...), custom_call_target="tpu_custom_call" | custom-call | tf_op jit(solution)/shard_map/remap_both_ways/pallas_call | solution.py:282
  46.9 18.9 %all_to_all.21.in_ref = bf16[8,224,128]{2,1,0:T(8,128)(2,1)S(1)} all-to-all(bf16[8,224,128]{2,1,0:T(8,128)(2,1)S(1)} %get-tuple-element.23), channel_id=1, replica_groups=mesh['grp'=96,'sub'=8] {'sub'}, dimensions={0} | all-to-all | bytes 917504 | tf_op jit(solution)/shard_map/all_to_all | solution.py:308
  65.9 0.7 total_group.1
  66.5 6.9 %all-to-all-start.2 = ((f32[96,2,128]{2,1,0:T(2,128)}), f32[96,2,128]{2,1,0:T(2,128)S(1)}, u32[]{:S(2)}, u32[]{:S(2)}) async-start(f32[96,2,128]{2,1,0:T(2,128)} %bitcast.6), calls=%async_computation.2 | async-start | bytes 196608 | tf_op jit(solution)/shard_map/all_to_all | solution.py:326
  73.4 0.1 split_routes.1
  73.5 3.5 %collective-permute-start.2 = (bf16[8,72,128]{2,1,0:T(8,128)(2,1)S(1)}, bf16[8,72,128]{2,1,0:T(8,128)(2,1)S(1)}, u32[]{:S(2)}, u32[]{:S(2)}) collective-permute-start(bf16[8,72,128]{2,1,0:T(8,128)(2,1)S(1)} %get-tuple-element.24), channel_id=1, source_target_pairs={{0,760},{8,16},{16,8},{24,32},{32,24},{40,48},{48,40},{56,64},{64,... | collective-permute-start | bytes 442376 | tf_op jit(solution)/shard_map/ppermute | solution.py:327
  77.1 5.9 %collective-permute-start.3 = (bf16[8,72,128]{2,1,0:T(8,128)(2,1)S(1)}, bf16[8,72,128]{2,1,0:T(8,128)(2,1)S(1)}, u32[]{:S(2)}, u32[]{:S(2)}) collective-permute-start(bf16[8,72,128]{2,1,0:T(8,128)(2,1)S(1)} %get-tuple-element.25), channel_id=1, source_target_pairs={{0,8},{8,0},{16,24},{24,16},{32,40},{40,32},{48,56},{56,48},{64,72... | collective-permute-start | bytes 442376 | tf_op jit(solution)/shard_map/ppermute | solution.py:328
  83.0 0.7 copy-done.1
  83.7 0.9 %collect_own.1 = (f32[33,8,128]{2,1,0:T(8,128)S(1)}, f32[33,8,128]{2,1,0:T(8,128)S(1)}) custom-call(s32[18,1,8]{2,1,0:T(1,128)S(1)} %bitcast.11, s32[3,1,8]{2,1,0:T(1,128)S(1)} %bitcast.13, bf16[8,72,128]{2,1,0:T(8,128)(2,1)S(1)} %get-tuple-element.26.own_ref), custom_call_target="tpu_custom_call" | custom-call | flops 1000000 | bytes 8000000 | tf_op jit(solution)/shard_map/collect_own/pallas_call | solution.py:331
  84.6 1.7 %collect_flux.1 = (bf16[12,4096]{1,0:T(8,128)(2,1)}, s32[8,128]{1,0:T(8,128)S(1)}) custom-call(s32[18,1,8]{2,1,0:T(1,128)S(1)} %bitcast.12, s32[3,1,8]{2,1,0:T(1,128)S(1)} %bitcast.14, bf16[8,72,128]{2,1,0:T(8,128)(2,1)S(1)} %collective-permute-done.2.chip_ref, bf16[8,72,128]{2,1,0:T(8,128)(2,1)S(1)} %collective-permute-done.3.core_ref, ...), custom_call_target="tpu_custom_call" | custom-call | flops 1000000 | bytes 8000000 | tf_op jit(solution)/shard_map/collect_flux/pallas_call | solution.py:340
  86.4 0.5 all-to-all-done.2
  86.9 0.5 total_all.1
  (8 shorter events, 0.0 us)
Async XLA Ops:
  2.5 18.4 %all-to-all-start = ((bf16[8,192,128]{2,1,0:T(8,128)(2,1)}), bf16[8,192,128]{2,1,0:T(8,128)(2,1)S(1)}, u32[]{:S(2)}, u32[]{:S(2)}) async-start(bf16[8,192,128]{2,1,0:T(8,128)(2,1)} %gather_slots.1), calls=%async_computation | async-start | bytes 786432 | tf_op jit(solution)/shard_map/all_to_all | solution.py:256
  21.0 62.0 %copy-start = (s32[1,3,8,6]{2,0,3,1:T(1,128)S(1)}, s32[1,3,8,6]{2,0,3,1:T(1,128)}, u32[]{:S(2)}) copy-start(s32[1,3,8,6]{2,0,3,1:T(1,128)} %param.16) | copy-start | bytes 1732
  21.0 23.2 %collective-permute-start = (bf16[8,64,128]{2,1,0:T(8,128)(2,1)S(1)}, bf16[8,64,128]{2,1,0:T(8,128)(2,1)S(1)}, u32[]{:S(2)}, u32[]{:S(2)}) collective-permute-start(bf16[8,64,128]{2,1,0:T(8,128)(2,1)S(1)} %get-tuple-element.19), channel_id=1, source_target_pairs={{0,760},{8,16},{16,8},{24,32},{32,24},{40,48},{48,40},{56,64},{64,... | collective-permute-start | bytes 393224 | tf_op jit(solution)/shard_map/ppermute | solution.py:278
  29.8 14.4 %collective-permute-start.1 = (bf16[8,64,128]{2,1,0:T(8,128)(2,1)S(1)}, bf16[8,64,128]{2,1,0:T(8,128)(2,1)S(1)}, u32[]{:S(2)}, u32[]{:S(2)}) collective-permute-start(bf16[8,64,128]{2,1,0:T(8,128)(2,1)S(1)} %get-tuple-element.20), channel_id=1, source_target_pairs={{0,8},{8,0},{16,24},{24,16},{32,40},{40,32},{48,56},{56,48},{64,72... | collective-permute-start | bytes 393224 | tf_op jit(solution)/shard_map/ppermute | solution.py:279
  66.5 20.4 %all-to-all-start.2 = ((f32[96,2,128]{2,1,0:T(2,128)}), f32[96,2,128]{2,1,0:T(2,128)S(1)}, u32[]{:S(2)}, u32[]{:S(2)}) async-start(f32[96,2,128]{2,1,0:T(2,128)} %bitcast.6), calls=%async_computation.2 | async-start | bytes 196608 | tf_op jit(solution)/shard_map/all_to_all | solution.py:326
  73.5 11.1 %collective-permute-start.2 = (bf16[8,72,128]{2,1,0:T(8,128)(2,1)S(1)}, bf16[8,72,128]{2,1,0:T(8,128)(2,1)S(1)}, u32[]{:S(2)}, u32[]{:S(2)}) collective-permute-start(bf16[8,72,128]{2,1,0:T(8,128)(2,1)S(1)} %get-tuple-element.24), channel_id=1, source_target_pairs={{0,760},{8,16},{16,8},{24,32},{32,24},{40,48},{48,40},{56,64},{64,... | collective-permute-start | bytes 442376 | tf_op jit(solution)/shard_map/ppermute | solution.py:327
  77.1 7.5 %collective-permute-start.3 = (bf16[8,72,128]{2,1,0:T(8,128)(2,1)S(1)}, bf16[8,72,128]{2,1,0:T(8,128)(2,1)S(1)}, u32[]{:S(2)}, u32[]{:S(2)}) collective-permute-start(bf16[8,72,128]{2,1,0:T(8,128)(2,1)S(1)} %get-tuple-element.25), channel_id=1, source_target_pairs={{0,8},{8,0},{16,24},{24,16},{32,40},{40,32},{48,56},{56,48},{64,72... | collective-permute-start | bytes 442376 | tf_op jit(solution)/shard_map/ppermute | solution.py:328
  83.0 0.7 copy-start.1
